TPU v7x, 32 devices: a whole 2x2x4 slice. The times are simulated.
32 devices in a mesh: leaf: 4 (over y, core), node: 8 (over z, x).
Axes of the slice: x: 2, y: 2, z: 4, core: 2. Of those that a mesh axis runs over, the one named last changes fastest.
Arguments:
- sources: bfloat16 [2048, 16384], P('node', 'leaf'), may hold values from -6 to 6
- block_inverse: bfloat16 [512, 16384], P(None, ('leaf', 'node')), may hold values from -0.25 to 0.25
- basis_left: bfloat16 [64, 16384], P(None, ('leaf', 'node')), may hold values from -0.09375 to 0.09375
- basis_right: bfloat16 [64, 16384], P(None, ('leaf', 'node')), may hold values from -0.75 to 0.75
- couple_in: bfloat16 [64, 16384], P(None, ('leaf', 'node')), may hold values from -0.09375 to 0.09375
- couple_out: bfloat16 [64, 16384], P(None, ('leaf', 'node')), may hold values from -0.5 to 0.5
- column_of_shot: int32 [2048], replicated, may hold values from 0 to 2047, each once
- cell_map: int32 [16384], P(('leaf', 'node')), may hold values from 0 to 16383
Outputs:
- solution: bfloat16 [2048, 16384], P(None, ('leaf', 'node'))
- gradient: float32 [16384], P('node')
Inputs may be any that keep to these rules, and one draw needn't show every extreme that they name: `column_of_shot`: a permutation of the 2048 column numbers.
All inputs are finite; a program needn't handle non-finite values.
Results may differ from a plain program's by a relative error of at most 0.02.
Values may be sent and summed in bfloat16 or wider, within the bound.
A program may use at most 64 MiB of HBM per device.

v0:
```python
import jax
import jax.numpy as jnp
from jax import lax
from jax.sharding import PartitionSpec as P

CELL_DEV = 2048


CONTRACT_LAST = (((1,), (1,)), ((), ()))


def passed_along(x, axis, by):
    count = lax.axis_size(axis)
    pairs = [(i, i + by) for i in range(count) if 0 <= i + by < count]
    return lax.ppermute(x, axis, pairs)


def project_rows(values, basis):
    return lax.dot_general(values, basis, CONTRACT_LAST, preferred_element_type=jnp.float32)


def per_device(
    sources, block_inverse, basis_left, basis_right, couple_in, couple_out, column_of_shot, cell_map
):
    shot_rows = lax.all_to_all(sources, "node", split_axis=1, concat_axis=0, tiled=True)
    total_cols = shot_rows.shape[0]
    inverse = (
        jnp.zeros((total_cols,), jnp.int32)
        .at[column_of_shot]
        .set(jnp.arange(total_cols, dtype=jnp.int32))
    )
    rhs_cols = jnp.take(shot_rows, inverse, axis=0)
    proj_rhs, proj_couple = lax.psum(
        (project_rows(rhs_cols, basis_left), project_rows(couple_in, basis_left)), "node"
    )
    fwd_rhs = (
        jnp.dot(rhs_cols, block_inverse, preferred_element_type=jnp.float32)
        + jnp.dot(proj_rhs.astype(jnp.bfloat16), basis_right, preferred_element_type=jnp.float32)
    ).astype(jnp.bfloat16)
    fwd_couple = (
        jnp.dot(couple_in, block_inverse, preferred_element_type=jnp.float32)
        + jnp.dot(proj_couple.astype(jnp.bfloat16), basis_right, preferred_element_type=jnp.float32)
    ).astype(jnp.bfloat16)
    carry_term = project_rows(fwd_rhs, couple_out)
    step_term = -project_rows(fwd_couple, couple_out)
    carry, step_map = lax.psum((carry_term, step_term), "node")
    incoming = jnp.zeros_like(carry)
    for relay_turn in range(lax.axis_size("leaf") - 1):
        incoming = passed_along(
            carry + jnp.dot(incoming, step_map, precision=lax.Precision.HIGHEST), "leaf", 1
        )
    forward = (
        fwd_rhs.astype(jnp.float32)
        - jnp.dot(incoming, fwd_couple.astype(jnp.float32), precision=lax.Precision.HIGHEST)
    ).astype(jnp.bfloat16)
    proj_fwd, proj_out = lax.psum(
        (project_rows(forward, basis_right), project_rows(couple_out, basis_right)), "node"
    )
    back_rhs = (
        lax.dot_general(forward, block_inverse, CONTRACT_LAST, preferred_element_type=jnp.float32)
        + jnp.dot(proj_fwd.astype(jnp.bfloat16), basis_left, preferred_element_type=jnp.float32)
    ).astype(jnp.bfloat16)
    back_couple = (
        lax.dot_general(
            couple_out, block_inverse, CONTRACT_LAST, preferred_element_type=jnp.float32
        )
        + jnp.dot(proj_out.astype(jnp.bfloat16), basis_left, preferred_element_type=jnp.float32)
    ).astype(jnp.bfloat16)
    lift_term = project_rows(back_rhs, couple_in)
    turn_term = -project_rows(back_couple, couple_in)
    lift, turn_map = (
        lax.psum(lift_term.astype(jnp.bfloat16), "node").astype(jnp.float32),
        lax.psum(turn_term.astype(jnp.bfloat16), "node").astype(jnp.float32),
    )
    returning = jnp.zeros_like(lift)
    for relay_turn in range(lax.axis_size("leaf") - 1):
        returning = passed_along(
            lift + jnp.dot(returning, turn_map, precision=lax.Precision.HIGHEST), "leaf", -1
        )
    solution = (
        back_rhs.astype(jnp.float32)
        - jnp.dot(returning, back_couple.astype(jnp.float32), precision=lax.Precision.HIGHEST)
    ).astype(jnp.bfloat16)
    corr = jnp.sum(solution.astype(jnp.float32) * forward.astype(jnp.float32), axis=0) / jnp.sqrt(
        jnp.float32(total_cols)
    )
    cell_count = CELL_DEV * lax.axis_size("node")
    partial_value = jnp.zeros((cell_count,), jnp.float32).at[cell_map].add(corr)
    totals = lax.psum(partial_value.astype(jnp.bfloat16), "leaf")
    gradient = lax.psum_scatter(totals, "node", scatter_dimension=0, tiled=True).astype(jnp.float32)
    return (solution, gradient)


def solution(mesh):
    return jax.shard_map(
        per_device,
        mesh=mesh,
        in_specs=(
            P("node", "leaf"),
            P(None, ("leaf", "node")),
            P(None, ("leaf", "node")),
            P(None, ("leaf", "node")),
            P(None, ("leaf", "node")),
            P(None, ("leaf", "node")),
            P(),
            P(("leaf", "node")),
        ),
        out_specs=(P(None, ("leaf", "node")), P("node")),
        check_vma=False,
    )
```

profile of v0, /device:TPU:0, one launch (start us, length us, event | category | flops | bytes accessed | tf_op | source)
XLA Modules:
  0.0 533.0 jit_solution(7067816113884990155)
XLA Ops:
  7.2 3.2 copy.14
  10.4 7.4 %all-to-all-start = ((bf16[256,8,512]{2,0,1:T(8,128)(2,1)}), bf16[256,8,512]{2,0,1:T(8,128)(2,1)S(1)}, u32[]{:S(2)}, u32[]{:S(2)}) async-start(bf16[256,8,512]{2,0,1:T(8,128)(2,1)} %bitcast.52), calls=%async_computation | async-start | bytes 4194304 | tf_op jit(solution)/shard_map/all_to_all | solution.py:25
  17.8 8.0 %scatter_custom_fusion = s32[2048]{0:T(1024)S(1)} fusion(s32[2048]{0:T(1024)S(1)} %compare_select_fusion.1, s32[2048]{0:T(1024)S(1)} %iota.3, s32[]{:T(128)} %constant.8.clone.1), kind=kCustom, calls=%fused_computation.41 | custom fusion | bytes 8196 | tf_op jit(solution)/shard_map/scatter | solution.py:30
  26.1 63.2 %psum.65 = bf16[64,64]{1,0:T(8,128)(2,1)S(1)} all-reduce(f32[64,64]{1,0:T(8,128)S(1)} %fusion.21), channel_id=1, replica_groups=mesh['leaf'=4,'node'=8] {'node'}, use_global_device_ids=true, to_apply=%region_3.4 | all-reduce | flops 4096 | bytes 24576 | tf_op jit(solution)/shard_map/psum | solution.py:33
  89.4 0.2 fusion
  89.8 9.2 %gather_fusion = bf16[2048,512]{1,0:T(8,128)(2,1)} fusion(bf16[2048,512]{1,0:T(8,128)(2,1)S(1)} %bitcast.51, s32[2048]{0:T(1024)S(1)} %fusion.14), kind=kCustom, calls=%fused_computation | custom fusion | bytes 4202496 | tf_op jit(solution)/shard_map/jit(_take)/gather | solution.py:32
  99.0 2.4 fusion.3
  101.4 2.9 fusion.4
  104.3 70.1 %all-reduce.11 = (bf16[2048,64]{1,0:T(8,128)(2,1)S(1)}, f32[64,64]{1,0:T(8,128)S(1)}) all-reduce(f32[2048,64]{1,0:T(8,128)S(1)} %fusion.3, f32[64,64]{1,0:T(8,128)S(1)} %convolution_negate_fusion.1), channel_id=1, replica_groups=mesh['leaf'=4,'node'=8] {'node'}, use_global_device_ids=true, to_apply=%region_1.2 | all-reduce | flops 135168 | bytes 819200 | tf_op jit(solution)/shard_map/psum | solution.py:33
  174.4 2.9 add_convert_fusion.1
  177.3 1.3 copy-done.1
  178.6 1.6 fusion.20
  180.2 72.5 %all-reduce.8.cloned.1.call-done = f32[2048,64]{0,1:T(8,128)} async-done(((f32[2048,64]{0,1:T(8,128)}), f32[2048,64]{0,1:T(8,128)}) %all-reduce.8.cloned.1.call-update) | async-done | bytes 524304 | tf_op jit(solution)/shard_map/psum | solution.py:46
  252.7 1.3 broadcast_add_fusion
  254.0 1.3 collective-permute-start
  255.3 1.5 collective-permute-done
  256.8 1.7 convolution_add_fusion.4
  258.5 8.7 %collective-permute-start.1 = (f32[2048,64]{0,1:T(8,128)S(1)}, f32[2048,64]{0,1:T(8,128)S(1)}, u32[]{:S(2)}, u32[]{:S(2)}) collective-permute-start(f32[2048,64]{0,1:T(8,128)S(1)} %convolution_add_fusion.4), channel_id=1, source_target_pairs={{0,8},{8,16},{16,24},{1,9},{9,17},{17,25},{2,10},{10,18},{18,26},{... | collective-permute-start | bytes 1572872 | tf_op jit(solution)/shard_map/ppermute | solution.py:15
  267.2 1.5 collective-permute-done.1
  268.7 0.6 convolution_add_fusion.3
  269.4 9.0 %collective-permute-start.2 = (f32[2048,64]{0,1:T(8,128)S(1)}, f32[2048,64]{0,1:T(8,128)S(1)}, u32[]{:S(2)}, u32[]{:S(2)}) collective-permute-start(f32[2048,64]{0,1:T(8,128)S(1)} %convolution_add_fusion.3), channel_id=1, source_target_pairs={{0,8},{8,16},{16,24},{1,9},{9,17},{17,25},{2,10},{10,18},{18,26},{... | collective-permute-start | bytes 1572872 | tf_op jit(solution)/shard_map/ppermute | solution.py:15
  278.5 1.3 collective-permute-done.2
  279.9 2.0 subtract_convert_fusion.1
  281.9 1.7 fusion.23
  283.5 3.2 fusion.22
  286.7 72.1 %all-reduce.12 = (bf16[2048,64]{1,0:T(8,128)(2,1)S(1)}, bf16[64,64]{1,0:T(8,128)(2,1)S(1)}) all-reduce(f32[2048,64]{1,0:T(8,128)} %fusion.23, f32[64,64]{1,0:T(8,128)S(1)} %fusion.24), channel_id=1, replica_groups=mesh['leaf'=4,'node'=8] {'node'}, use_global_device_ids=true, to_apply=%region_6.7 | all-reduce | flops 135168 | bytes 811008 | tf_op jit(solution)/shard_map/psum | solution.py:56
  358.8 2.9 add_convert_fusion
  361.7 1.3 copy-done.3
  363.0 1.5 convolution_convert_fusion
  364.7 0.3 fusion.1
  364.9 0.1 fusion.2
  365.1 35.5 %psum.70 = bf16[64,64]{1,0:T(8,128)(2,1)S(1)} all-reduce(bf16[64,64]{1,0:T(8,128)(2,1)S(1)} %fusion.2), channel_id=1, replica_groups=mesh['leaf'=4,'node'=8] {'node'}, use_global_device_ids=true, to_apply=%region_9.10 | all-reduce | flops 4096 | bytes 16384 | tf_op jit(solution)/shard_map/psum | solution.py:73
  400.6 42.0 %all-reduce.10.cloned.1.call-done = bf16[2048,64]{0,1:T(8,128)(2,1)} async-done(((bf16[2048,64]{0,1:T(8,128)(2,1)}), bf16[2048,64]{0,1:T(8,128)(2,1)}) %all-reduce.10.cloned.1.call-update) | async-done | bytes 262160 | tf_op jit(solution)/shard_map/psum | solution.py:72
  442.6 1.3 convolution_add_fusion.2
  444.0 1.3 collective-permute-start.3
  445.3 2.5 collective-permute-done.3
  447.8 1.4 convolution_add_fusion.1
  449.1 1.3 collective-permute-start.4
  450.4 8.6 %collective-permute-done.4 = f32[2048,64]{0,1:T(8,128)S(1)} collective-permute-done((f32[2048,64]{0,1:T(8,128)S(1)}, f32[2048,64]{0,1:T(8,128)S(1)}, u32[]{:S(2)}, u32[]{:S(2)}) %collective-permute-start.4) | collective-permute-done | bytes 524320 | tf_op jit(solution)/shard_map/ppermute | solution.py:15
  459.0 1.2 convolution_add_fusion
  460.2 1.3 collective-permute-start.5
  461.5 0.6 dynamic-slice
  462.8 8.1 %collective-permute-done.5 = f32[2048,64]{0,1:T(8,128)S(1)} collective-permute-done((f32[2048,64]{0,1:T(8,128)}, f32[2048,64]{0,1:T(8,128)S(1)}, u32[]{:S(2)}, u32[]{:S(2)}) %collective-permute-start.5) | collective-permute-done | bytes 524320 | tf_op jit(solution)/shard_map/ppermute | solution.py:15
  470.9 5.3 multiply_reduce_fusion
  476.3 3.3 scatter_custom_fusion.1
  479.6 35.4 %all-reduce = bf16[16384]{0:T(1024)(128)(2,1)S(1)} all-reduce(bf16[16384]{0:T(1024)(128)(2,1)S(1)} %convert_element_type.77), channel_id=2, replica_groups=mesh['leaf'=4,'node'=8] {'node'}, use_global_device_ids=true, to_apply=%region_13.14.clone | all-reduce | flops 16384 | bytes 65536
  515.0 10.6 %psum.72 = bf16[2048]{0:T(1024)(128)(2,1)S(1)} all-reduce(bf16[2048]{0:T(1024)(128)(2,1)S(1)} %dynamic-slice.1), channel_id=1, replica_groups=mesh['leaf'=4,'node'=8] {'leaf'}, use_global_device_ids=true, to_apply=%region_12.13 | all-reduce | flops 2048 | bytes 8192 | tf_op jit(solution)/shard_map/psum | solution.py:89
  525.6 0.6 convert_element_type.78
  (45 shorter events, 0.9 us)
Async XLA Ops:
  7.2 82.2 %copy-start = (bf16[512,512]{1,0:T(8,128)(2,1)S(1)}, bf16[512,512]{1,0:T(8,128)(2,1)}, u32[]{:S(2)}) copy-start(bf16[512,512]{1,0:T(8,128)(2,1)} %param.9) | copy-start | bytes 1572868
  10.3 7.5 %copy-start.11 = (s32[2048]{0:T(1024)S(1)}, s32[2048]{0:T(1024)}, u32[]{:S(2)}) copy-start(s32[2048]{0:T(1024)} %param.14) | copy-start | bytes 24580
  10.3 15.6 %copy-start.8 = (bf16[64,512]{1,0:T(8,128)(2,1)S(1)}, bf16[64,512]{1,0:T(8,128)(2,1)}, u32[]{:S(2)}) copy-start(bf16[64,512]{1,0:T(8,128)(2,1)} %param.12) | copy-start | bytes 196612
  10.4 15.6 %copy-start.10 = (bf16[64,512]{1,0:T(8,128)(2,1)S(1)}, bf16[64,512]{1,0:T(8,128)(2,1)}, u32[]{:S(2)}) copy-start(bf16[64,512]{1,0:T(8,128)(2,1)} %param.10) | copy-start | bytes 196612
  10.4 78.9 %copy-start.7 = (bf16[64,512]{1,0:T(8,128)(2,1)S(1)}, bf16[64,512]{1,0:T(8,128)(2,1)}, u32[]{:S(2)}) copy-start(bf16[64,512]{1,0:T(8,128)(2,1)} %param.11) | copy-start | bytes 196612
  10.4 79.3 %copy-start.9 = (bf16[64,512]{1,0:T(8,128)(2,1)S(1)}, bf16[64,512]{1,0:T(8,128)(2,1)}, u32[]{:S(2)}) copy-start(bf16[64,512]{1,0:T(8,128)(2,1)} %param.13) | copy-start | bytes 196612
  10.4 79.4 %all-to-all-start = ((bf16[256,8,512]{2,0,1:T(8,128)(2,1)}), bf16[256,8,512]{2,0,1:T(8,128)(2,1)S(1)}, u32[]{:S(2)}, u32[]{:S(2)}) async-start(bf16[256,8,512]{2,0,1:T(8,128)(2,1)} %bitcast.52), calls=%async_computation | async-start | bytes 4194304 | tf_op jit(solution)/shard_map/all_to_all | solution.py:25
  17.8 234.9 %all-reduce.8.cloned.1.call-start = ((), (), s32[]{:S(2)}) async-start(), calls=%async_computation.1 | async-start | bytes 1048576 | tf_op jit(solution)/shard_map/psum | solution.py:46
  99.0 2.4 copy-start.6
  177.3 1.3 copy-start.1
  180.2 262.5 %all-reduce.10.cloned.1.call-start = ((), (), s32[]{:S(2)}) async-start(), calls=%async_computation.2 | async-start | bytes 524288 | tf_op jit(solution)/shard_map/psum | solution.py:72
  252.7 16.0 %copy-start.4 = (f32[2048,64]{0,1:T(8,128)S(1)}, f32[2048,64]{0,1:T(8,128)}, u32[]{:S(2)}) copy-start(f32[2048,64]{0,1:T(8,128)} %all-reduce.8.cloned.1.call-done) | copy-start | bytes 1572868
  252.7 27.1 %copy-start.2 = (bf16[2048,512]{1,0:T(8,128)(2,1)S(1)}, bf16[2048,512]{1,0:T(8,128)(2,1)}, u32[]{:S(2)}) copy-start(bf16[2048,512]{1,0:T(8,128)(2,1)} %copy-done.1) | copy-start | bytes 6291460
  254.0 2.8 collective-permute-start
  258.5 10.2 %collective-permute-start.1 = (f32[2048,64]{0,1:T(8,128)S(1)}, f32[2048,64]{0,1:T(8,128)S(1)}, u32[]{:S(2)}, u32[]{:S(2)}) collective-permute-start(f32[2048,64]{0,1:T(8,128)S(1)} %convolution_add_fusion.4), channel_id=1, source_target_pairs={{0,8},{8,16},{16,24},{1,9},{9,17},{17,25},{2,10},{10,18},{18,26},{... | collective-permute-start | bytes 1572872 | tf_op jit(solution)/shard_map/ppermute | solution.py:15
  269.4 10.5 %collective-permute-start.2 = (f32[2048,64]{0,1:T(8,128)S(1)}, f32[2048,64]{0,1:T(8,128)S(1)}, u32[]{:S(2)}, u32[]{:S(2)}) collective-permute-start(f32[2048,64]{0,1:T(8,128)S(1)} %convolution_add_fusion.3), channel_id=1, source_target_pairs={{0,8},{8,16},{16,24},{1,9},{9,17},{17,25},{2,10},{10,18},{18,26},{... | collective-permute-start | bytes 1572872 | tf_op jit(solution)/shard_map/ppermute | solution.py:15
  361.7 1.3 copy-start.3
  364.6 96.9 %copy-start.13 = (u32[32]{0:T(128)S(1)}, u32[32]{0:T(128)}, u32[]{:S(2)}) copy-start(u32[32]{0:T(128)} %constant.31) | copy-start | bytes 388
  364.6 98.1 %copy-start.12 = (s32[512]{0:T(512)S(1)}, s32[512]{0:T(512)}, u32[]{:S(2)}) copy-start(s32[512]{0:T(512)} %param.15) | copy-start | bytes 6148
  442.6 16.4 %copy-start.5 = (bf16[2048,64]{0,1:T(8,128)(2,1)S(1)}, bf16[2048,64]{0,1:T(8,128)(2,1)}, u32[]{:S(2)}) copy-start(bf16[2048,64]{0,1:T(8,128)(2,1)} %all-reduce.10.cloned.1.call-done) | copy-start | bytes 786436
  444.0 3.8 collective-permute-start.3
  449.1 9.9 %collective-permute-start.4 = (f32[2048,64]{0,1:T(8,128)S(1)}, f32[2048,64]{0,1:T(8,128)S(1)}, u32[]{:S(2)}, u32[]{:S(2)}) collective-permute-start(f32[2048,64]{0,1:T(8,128)S(1)} %convolution_add_fusion.1), channel_id=1, source_target_pairs={{8,0},{16,8},{24,16},{9,1},{17,9},{25,17},{10,2},{18,10},{26,18},{... | collective-permute-start | bytes 1572872 | tf_op jit(solution)/shard_map/ppermute | solution.py:15
  460.2 10.7 %collective-permute-start.5 = (f32[2048,64]{0,1:T(8,128)}, f32[2048,64]{0,1:T(8,128)S(1)}, u32[]{:S(2)}, u32[]{:S(2)}) collective-permute-start(f32[2048,64]{0,1:T(8,128)} %convolution_add_fusion), channel_id=1, source_target_pairs={{8,0},{16,8},{24,16},{9,1},{17,9},{25,17},{10,2},{18,10},{26,18},{... | collective-permute-start | bytes 1572872 | tf_op jit(solution)/shard_map/ppermute | solution.py:15
Sparse Core Ops, SparseCore 0:
  180.3 72.3 all-reduce.7
  364.6 77.9 all-reduce.9
where the time goes:
time: 534 us; the launch traced here: 533 us
  blocking collectives  287 us (54%)
  waiting for transfers between devices  138 us (26%)
  matrix products  33.7 us (6%)
  starting transfers between devices  30.4 us (6%)
  local copies, waits for them, and re-layouts  23.7 us (4%)
  between operations  15.1 us (3%)
    psum x2, blocking collectives, per_device(): lax.psum((project_rows(rhs_cols, basis_left), project_rows(couple_in, bas...  133 us
    psum x1, waiting for transfers between devices, per_device(): carry, step_map = lax.psum((carry_term, step_term), 'node')  72.5 us
    psum x1, blocking collectives, per_device(): lax.psum((project_rows(forward, basis_right), project_rows(couple_out, ba...  72.1 us
    psum x1, waiting for transfers between devices, per_device(): lax.psum(lift_term.astype(jnp.bfloat16), 'node').astype(jnp.float32)  42 us
    psum x1, blocking collectives, per_device(): lax.psum(turn_term.astype(jnp.bfloat16), 'node').astype(jnp.float32)  35.5 us
    unnamed x1, blocking collectives  35.4 us
    ppermute x6, waiting for transfers between devices, passed_along(): return lax.ppermute(x, axis, pairs)  23.5 us
    ppermute x6, starting transfers between devices, passed_along(): return lax.ppermute(x, axis, pairs)  22.9 us
  transfers between devices with their start and end apart: 9, of which 8 were waited for; matrix products, arithmetic and copies ran while one was open for 2% of the time, Pallas kernels for 0%

commit v1 on v0

v1 whole, which is shorter than its diff:
```python
import functools

import jax
import jax.numpy as jnp
from jax import lax
from jax.experimental import pallas as pl
from jax.experimental.pallas import tpu as pltpu
from jax.sharding import PartitionSpec as P

CELL_DEV = 2048
LANES = 128
MESH = pl.DeviceIdType.MESH


def dot_rows(a, b):
    return lax.dot_general(a, b, (((1,), (1,)), ((), ())), preferred_element_type=jnp.float32)


def dot(a, b):
    return jnp.dot(a, b, preferred_element_type=jnp.float32)


def half(x):
    return x.astype(jnp.bfloat16)


class Tree:
    def __init__(self, buf, zsend, xsend, recv, leaf, node, zs, xs):
        self.buf, self.zsend, self.xsend, self.recv = buf, zsend, xsend, recv
        self.leaf, self.zs, self.xs = leaf, zs, xs
        self.z, self.x = node // xs, node % xs

    def copy(self, slot, dst, sem):
        return pltpu.make_async_remote_copy(
            src_ref=self.buf.at[slot],
            dst_ref=self.buf.at[slot],
            send_sem=sem,
            recv_sem=self.recv.at[slot],
            device_id=(self.leaf, dst),
            device_id_type=MESH,
        )

    def slot(self, zz):
        return zz * self.xs + self.x

    def up(self, zz, sem):
        return self.copy(self.slot(zz), (self.z + 1) * self.xs + self.x, self.zsend.at[sem])

    def down(self, zz, sem):
        return self.copy(self.slot(zz), (self.z - 1) * self.xs + self.x, self.zsend.at[sem])

    def across(self, zz):
        return [
            self.copy(
                self.slot(zz),
                self.z * self.xs + (self.x + i) % self.xs,
                self.xsend.at[zz * (self.xs - 1) + i - 1],
            )
            for i in range(1, self.xs)
        ]

    def start(self):
        pl.when(self.z + 1 < self.zs)(lambda: self.up(self.z, self.z).start())
        pl.when(self.z > 0)(lambda: self.down(self.z, self.zs).start())
        for c in self.across(self.z):
            c.start()

    def wait_slot(self, slot):
        self.copy(slot, 0, self.zsend.at[0]).wait_recv()

    def relay(self, hop, use):
        below, above = self.z - hop, self.z + hop

        @pl.when(below >= 0)
        def _():
            self.wait_slot(self.slot(below))
            pl.when(self.z + 1 < self.zs)(lambda: self.up(below, below).start())
            for c in self.across(below):
                c.start()

        @pl.when(above < self.zs)
        def _():
            self.wait_slot(self.slot(above))
            pl.when(self.z > 0)(lambda: self.down(above, above).start())
            for c in self.across(above):
                c.start()

        if use is not None:
            pl.when(below >= 0)(lambda: use(self.slot(below)))
            pl.when(above < self.zs)(lambda: use(self.slot(above)))

    def partners(self, use):
        for i in range(1, self.xs):
            @pl.loop(0, self.zs)
            def _(zz):
                slot = zz * self.xs + (self.x + i) % self.xs
                self.wait_slot(slot)
                if use is not None:
                    use(slot)

    def finish(self):
        @pl.loop(0, self.zs)
        def _(zz):
            for c in self.across(zz):
                c.wait_send()
            pl.when((zz <= self.z) & (self.z + 1 < self.zs))(
                lambda: self.up(zz, zz).wait_send()
            )
            pl.when((zz > self.z) & (self.z > 0))(lambda: self.down(zz, zz).wait_send())
        pl.when(self.z > 0)(lambda: self.down(self.z, self.zs).wait_send())


def kernel(
    n, leaves, xs,
    src, b_ref, bl_ref, br_ref, ci_ref, co_ref, shot_ref, cell_ref,
    sol_ref, grad_ref,
    src_v, rg, rhs, lg, cg, onehot, zacc, u_ref, t_ref, gpart, gbuf, lbuf,
    src_sem, own_sem, rz, rx, rr, a_send, a_recv, l_send, l_recv, cz, cx, cr,
    g_send, g_recv, h_send, h_recv,
):
    leaf, node = lax.axis_index("leaf"), lax.axis_index("node")
    zs = n // xs
    k, block = bl_ref.shape
    shots = src.shape[0]
    total = n * shots

    barrier = pltpu.get_barrier_semaphore()

    @pl.loop(1, n)
    def _(i):
        pl.semaphore_signal(
            barrier, inc=1, device_id=(leaf, (node + i) % n), device_id_type=MESH
        )

    @pl.loop(1, leaves)
    def _(i):
        pl.semaphore_signal(
            barrier, inc=1, device_id=((leaf + i) % leaves, node), device_id_type=MESH
        )

    src_copy = pltpu.make_async_copy(src, src_v, src_sem)
    src_copy.start()

    def columns(j):
        return pl.ds(pl.multiple_of(j * block, block), block)

    own_copy = pltpu.make_async_copy(src.at[:, columns(node)], rhs.at[node], own_sem)
    own_copy.start()

    b = b_ref[...]
    u = dot(ci_ref[...], b)
    u_ref[...] = u
    stacked = jnp.concatenate([co_ref[...], br_ref[...], half(u)], axis=0)
    t = dot_rows(stacked, b)
    t_ref[...] = t[:k]
    v = jnp.concatenate([bl_ref[...], half(t)], axis=0)
    rg[node, : 4 * k] = v
    rg[node, 4 * k :, : 4 * k] = half(dot_rows(ci_ref[...], v))
    rg[node, 4 * k :, 4 * k : 8 * k] = half(
        dot_rows(br_ref[...], jnp.concatenate([bl_ref[...], stacked], axis=0))
    )

    pl.semaphore_wait(barrier, n - 1 + leaves - 1)

    basis = Tree(rg, rz, rx, rr, leaf, node, zs, xs)
    basis.start()

    def shot_copy(j):
        return pltpu.make_async_remote_copy(
            src_ref=src.at[:, columns(j)],
            dst_ref=rhs.at[node],
            send_sem=a_send.at[j],
            recv_sem=a_recv.at[node],
            device_id=(leaf, j),
            device_id_type=MESH,
        )

    @pl.loop(1, n)
    def _(i):
        shot_copy((node + i) % n).start()

    rows_at = 256

    @pl.loop(0, n)
    def _(j):
        @pl.loop(0, total // rows_at)
        def _(r):
            at = pl.multiple_of(r * rows_at, rows_at)
            row = lax.broadcasted_iota(jnp.int32, (rows_at, shots), 0) + at
            onehot[j, pl.ds(at, rows_at), :] = half(jnp.where(row == shot_ref[j], 1.0, 0.0))

    src_copy.wait()
    zacc[...] = dot_rows(src_v[:, columns(node)], rg[node, : 4 * k])

    def project(slot):
        zacc[...] += dot_rows(src_v[:, columns(slot)], rg[slot, : 4 * k])

    for hop in range(1, zs):
        basis.relay(hop, project)
    basis.partners(project)

    s = rg[0, 4 * k :, :].astype(jnp.float32)
    for j in range(1, n):
        s = s + rg[j, 4 * k :, :].astype(jnp.float32)
    s3t = half(s[:, :k])
    ss = half(s[:, 4 * k : 8 * k])
    f = s[:, : 4 * k] + dot(s3t, ss)
    z = zacc[...]
    proj = half(z[:, :k])
    zf = z + dot(proj, ss)
    carry, z2, z3 = zf[:, k : 2 * k], zf[:, 2 * k : 3 * k], zf[:, 3 * k :]
    fb = f[:, 2 * k : 3 * k]
    lift = z3 + dot_rows(half(z2), s3t)
    lift_map = f[:, 3 * k :] + dot_rows(half(fb), s3t)
    lg[leaf, :shots] = half(jnp.concatenate([carry, lift], axis=1))
    lg[leaf, shots:] = half(-jnp.concatenate([f[:, k : 2 * k], lift_map], axis=1))

    def leaf_copy(i):
        return pltpu.make_async_remote_copy(
            src_ref=lg.at[leaf],
            dst_ref=lg.at[leaf],
            send_sem=l_send.at[i],
            recv_sem=l_recv.at[leaf],
            device_id=((leaf + i) % leaves, node),
            device_id_type=MESH,
        )

    for i in range(1, leaves):
        leaf_copy(i).start()

    fc = half(u_ref[...] + dot(s3t, br_ref[...]))
    s1 = half(s[:, 5 * k : 6 * k])
    bc = half(
        t_ref[...]
        + lax.dot_general(s1, bl_ref[...], (((0,), (0,)), ((), ())), preferred_element_type=jnp.float32)
    )
    fwd_low = jnp.concatenate([br_ref[...], fc], axis=0)
    back_low = jnp.concatenate([bl_ref[...], bc], axis=0)

    for i in range(1, leaves):
        j = (leaf + i) % leaves
        pltpu.make_async_remote_copy(
            src_ref=lg.at[leaf], dst_ref=lg.at[j], send_sem=l_send.at[0],
            recv_sem=l_recv.at[j], device_id=(j, node), device_id_type=MESH,
        ).wait_recv()

    incoming = jnp.zeros((shots, k), jnp.float32)
    own_in = jnp.zeros((shots, k), jnp.float32)
    lifts = []
    for g in range(leaves):
        own_in = jnp.where(leaf == g, incoming, own_in)
        both = lg[g, :shots].astype(jnp.float32)
        if g > 0:
            both = both + dot(half(incoming), lg[g, shots:])
        incoming = both[:, :k]
        lifts.append(both[:, k:])
    returning = jnp.zeros((shots, k), jnp.float32)
    own_ret = jnp.zeros((shots, k), jnp.float32)
    for g in range(leaves - 1, -1, -1):
        own_ret = jnp.where(leaf == g, returning, own_ret)
        if g < leaves - 1:
            returning = lifts[g] + dot_rows(half(returning), lg[g, shots:, :k])
        else:
            returning = lifts[g]
    proj_fwd = z2 - dot(half(own_in), half(fb))
    cg[node] = half(
        jnp.concatenate([z[:, :k], -own_in, proj_fwd, -own_ret], axis=1)
    )

    coefs = Tree(cg, cz, cx, cr, leaf, node, zs, xs)
    coefs.start()
    for hop in range(1, zs):
        coefs.relay(hop, None)
    coefs.partners(None)

    own_copy.wait()
    sums = jnp.zeros((1, block), jnp.float32)

    def shot_block(j, sums, first):
        low = cg[j]
        fwd = half(dot(rhs[j], b_ref[...]) + dot(low[:, : 2 * k], fwd_low))
        sol = half(dot_rows(fwd, b_ref[...]) + dot(low[:, 2 * k :], back_low))

        @pl.loop(0, total // rows_at)
        def _(r):
            rows = pl.ds(pl.multiple_of(r * rows_at, rows_at), rows_at)
            part = half(dot(onehot[j, rows, :], sol))
            if first:
                sol_ref[rows, :] = part
            else:
                sol_ref[rows, :] += part

        return sums + jnp.sum(
            sol.astype(jnp.float32) * fwd.astype(jnp.float32), axis=0, keepdims=True
        )

    sums = shot_block(node, sums, True)

    def later(i, sums):
        j = (node + n - i) % n
        pltpu.make_async_remote_copy(
            src_ref=rhs.at[j], dst_ref=rhs.at[j], send_sem=a_send.at[j],
            recv_sem=a_recv.at[j], device_id=(leaf, j), device_id_type=MESH,
        ).wait_recv()
        return shot_block(j, sums, False)

    sums = lax.fori_loop(1, n, later, sums)
    corr = sums / jnp.sqrt(jnp.float32(total))

    cell = cell_ref[...]
    slab = gpart.shape[1]
    high = lax.broadcasted_iota(jnp.int32, (n * slab, block), 0) == cell // LANES
    low_hit = lax.broadcasted_iota(jnp.int32, (LANES, block), 0) == cell % LANES
    placed = lax.dot_general(
        jnp.where(high, corr, 0.0),
        jnp.where(low_hit, 1.0, 0.0),
        (((1,), (1,)), ((), ())),
        preferred_element_type=jnp.float32,
        precision=lax.Precision.HIGHEST,
    )
    gpart[...] = placed.reshape(gpart.shape)

    def slab_copy(j, frm):
        return pltpu.make_async_remote_copy(
            src_ref=gpart.at[j], dst_ref=gbuf.at[frm], send_sem=g_send.at[j],
            recv_sem=g_recv.at[frm], device_id=(leaf, j), device_id_type=MESH,
        )

    @pl.loop(1, n)
    def _(i):
        slab_copy((node + i) % n, node).start()

    own = gpart[node]

    def add_slab(i, acc):
        j = (node + n - i) % n
        slab_copy(j, j).wait_recv()
        return acc + gbuf[j]

    own = lax.fori_loop(1, n, add_slab, own)
    lbuf[leaf] = own

    def grad_copy(i, frm):
        return pltpu.make_async_remote_copy(
            src_ref=lbuf.at[leaf], dst_ref=lbuf.at[frm], send_sem=h_send.at[i],
            recv_sem=h_recv.at[frm], device_id=((leaf + i) % leaves, node),
            device_id_type=MESH,
        )

    for i in range(1, leaves):
        grad_copy(i, leaf).start()
    for i in range(1, leaves):
        grad_copy(i, (leaf + leaves - i) % leaves).wait_recv()
    acc = lbuf[0]
    for g in range(1, leaves):
        acc = acc + lbuf[g]
    grad_ref[...] = acc

    basis.finish()
    coefs.finish()
    for i in range(1, leaves):
        leaf_copy(i).wait_send()
        grad_copy(i, leaf).wait_send()

    @pl.loop(1, n)
    def _(i):
        j = (node + i) % n
        shot_copy(j).wait_send()
        slab_copy(j, node).wait_send()


def per_device(n, leaves, sources, block_inverse, basis_left, basis_right, couple_in, couple_out, column_of_shot, cell_map):
    xs = max(d for d in range(1, n + 1) if n % d == 0 and (2 * d * d <= n or d == 1))
    zs = n // xs
    k, block = basis_left.shape
    shots = sources.shape[0]
    total = n * shots
    slab = CELL_DEV // LANES
    bf16, f32 = jnp.bfloat16, jnp.float32
    dma = pltpu.SemaphoreType.DMA
    vmem = pl.BlockSpec(memory_space=pltpu.VMEM)
    solution_out, grad = pl.pallas_call(
        functools.partial(kernel, n, leaves, xs),
        out_shape=(
            jax.ShapeDtypeStruct((total, block), bf16),
            jax.ShapeDtypeStruct((slab, LANES), f32),
        ),
        in_specs=[pl.BlockSpec(memory_space=pl.ANY)] + [vmem] * 7,
        out_specs=(vmem, vmem),
        scratch_shapes=[
            pltpu.VMEM(sources.shape, bf16),
            pltpu.VMEM((n, 5 * k, block), bf16),
            pltpu.VMEM((n, shots, block), bf16),
            pltpu.VMEM((leaves, shots + k, 2 * k), bf16),
            pltpu.VMEM((n, shots, 4 * k), bf16),
            pltpu.VMEM((n, total, shots), bf16),
            pltpu.VMEM((shots, 4 * k), f32),
            pltpu.VMEM((k, block), f32),
            pltpu.VMEM((k, block), f32),
            pltpu.VMEM((n, slab, LANES), f32),
            pltpu.VMEM((n, slab, LANES), f32),
            pltpu.VMEM((leaves, slab, LANES), f32),
            dma, dma,
            dma((zs + 1,)), dma((max(zs * (xs - 1), 1),)), dma((n,)),
            dma((n,)), dma((n,)),
            dma((leaves,)), dma((leaves,)),
            dma((zs + 1,)), dma((max(zs * (xs - 1), 1),)), dma((n,)),
            dma((n,)), dma((n,)),
            dma((leaves,)), dma((leaves,)),
        ],
        compiler_params=pltpu.CompilerParams(
            collective_id=0, has_side_effects=True, vmem_limit_bytes=56 * 1024 * 1024
        ),
    )(
        sources, block_inverse, basis_left, basis_right, couple_in, couple_out,
        column_of_shot.reshape(n, 1, shots), cell_map.reshape(1, -1),
    )
    return solution_out, grad.reshape(-1)


def solution(mesh):
    both = P(None, ("leaf", "node"))
    return jax.shard_map(
        functools.partial(per_device, mesh.shape["node"], mesh.shape["leaf"]),
        mesh=mesh,
        in_specs=(P("node", "leaf"), both, both, both, both, both, P(), P(("leaf", "node"))),
        out_specs=(both, P("node")),
        check_vma=False,
    )
```

time: 534 us -> 140 us (0.26)
  blocking collectives: 287 us -> 0 us
  waiting for transfers between devices: 138 us -> 0 us
  Pallas kernels: 0 us -> 136 us
  matrix products: 33.7 us -> 0 us
  starting transfers between devices: 30.4 us -> 0 us
  local copies, waits for them, and re-layouts: 23.7 us -> 3.65 us
  between operations: 15.1 us -> 0.65 us
    psum x5 -> x0, blocking collectives: 251 us -> none  [the longest x2 133 us: per_device(): lax.psum((project_rows(rhs_cols, basis_left), project_rows(couple_in, bas...]
    pallas_call x0 -> x1, Pallas kernels: none -> 136 us  [per_device(): pl.pallas_call(functools.partial(kernel, n, leaves, xs), out_shape=(jax.S...]
    psum x2 -> x0, waiting for transfers between devices: 114 us -> none  [the longest x1 72.5 us: per_device(): carry, step_map = lax.psum((carry_term, step_term), 'node')]
    unnamed x1 -> x0, blocking collectives: 35.4 us -> none
    dot_general x23 -> x0, matrix products: 33.7 us -> none  [the longest x8 7.62 us: project_rows(): lax.dot_general(values, basis, CONTRACT_LAST, preferred_element_type=jnp....]
    ppermute x6 -> x0, waiting for transfers between devices: 23.5 us -> none  [passed_along(): return lax.ppermute(x, axis, pairs)]
    ppermute x6 -> x0, starting transfers between devices: 22.9 us -> none  [passed_along(): return lax.ppermute(x, axis, pairs)]
    gather x1 -> x0, local copies, waits for them, and re-layouts: 9.21 us -> none  [per_device(): rhs_cols = jnp.take(shot_rows, inverse, axis=0)]
  transfers between devices with their start and end apart: 9 -> 0, of which waited for: 8 -> 0; matrix products, arithmetic and copies ran while one was open for 2% -> 0% of each run, Pallas kernels for 0% -> 0%
where the time goes in v1:
time: 140 us
  Pallas kernels  136 us (97%)
  local copies, waits for them, and re-layouts  3.65 us (3%)
    pallas_call x1, Pallas kernels, per_device(): pl.pallas_call(functools.partial(kernel, n, leaves, xs), out_shape=(jax.S...  136 us
    unnamed x4, local copies, waits for them, and re-layouts  3.65 us

profile of v1, /device:TPU:0, one launch (start us, length us, event | category | flops | bytes accessed | tf_op | source)
XLA Modules:
  0.0 139.9 jit_solution(10567172114328635845)
XLA Ops:
  0.6 135.6 %shard_map.95 = (bf16[2048,512]{1,0:T(8,128)(2,1)}, f32[16,128]{1,0:T(8,128)}) custom-call(bf16[256,4096]{1,0:T(8,128)(2,1)} %src.1, bf16[512,512]{1,0:T(8,128)(2,1)} %b_ref.1, bf16[64,512]{1,0:T(8,128)(2,1)} %bl_ref.1, bf16[64,512]{1,0:T(8,128)(2,1)} %br_ref.1, bf16[64,512]{1,0:T(8,128)(2,1)} %ci_ref.1, bf16[64,512]{1,0:T(8,128)(2,1)} %co_ref.1, ...), custom_call_target="tpu_custom_call" | custom-call | tf_op jit(solution)/shard_map/pallas_call | solution.py:382
  136.3 0.0 copy-start
  136.3 3.0 %copy.12 = bf16[2048,512]{1,0:T(8,128)(2,1)} copy(bf16[2048,512]{1,0:T(8,128)(2,1)} %get-tuple-element.8) | data formatting | bytes 4194304
  139.3 0.0 copy-done
  139.3 0.6 copy.13
Async XLA Ops:
  136.3 3.1 %copy-start = (f32[16,128]{1,0:T(8,128)S(1)}, f32[16,128]{1,0:T(8,128)}, u32[]{:S(2)}) copy-start(f32[16,128]{1,0:T(8,128)} %get-tuple-element.5) | copy-start | bytes 24580

commit v2 on v1

--- a/solution.py
+++ b/solution.py
@@ -175,9 +175,19 @@
             device_id_type=MESH,
         )
 
-    @pl.loop(1, n)
-    def _(i):
-        shot_copy((node + i) % n).start()
+    def peer(i, sign):
+        z, x = node // xs, node % xs
+        over = (i - zs) // zs + 1
+        same = ((z + sign * i + zs) % zs) * xs + x
+        cross = ((z + sign * (i % zs) + zs) % zs) * xs + (x + sign * over + xs) % xs
+        return jnp.where(i < zs, same, cross)
+
+    def send_shots(first, last):
+        @pl.loop(first, last)
+        def _(i):
+            shot_copy(peer(i, 1)).start()
+
+    send_shots(1, 2)
 
     rows_at = 256
 
@@ -197,6 +207,10 @@
 
     for hop in range(1, zs):
         basis.relay(hop, project)
+        if hop + 1 < zs:
+            send_shots(hop + 1, hop + 2)
+    crossing = n - zs
+    send_shots(zs, zs + crossing // 4)
     basis.partners(project)
 
     s = rg[0, 4 * k :, :].astype(jnp.float32)
@@ -227,6 +241,7 @@
 
     for i in range(1, leaves):
         leaf_copy(i).start()
+    send_shots(zs + crossing // 4, zs + crossing // 2)
 
     fc = half(u_ref[...] + dot(s3t, br_ref[...]))
     s1 = half(s[:, 5 * k : 6 * k])
@@ -271,6 +286,7 @@
     coefs.start()
     for hop in range(1, zs):
         coefs.relay(hop, None)
+    send_shots(zs + crossing // 2, n)
     coefs.partners(None)
 
     own_copy.wait()
@@ -297,7 +313,7 @@
     sums = shot_block(node, sums, True)
 
     def later(i, sums):
-        j = (node + n - i) % n
+        j = peer(i, -1)
         pltpu.make_async_remote_copy(
             src_ref=rhs.at[j], dst_ref=rhs.at[j], send_sem=a_send.at[j],
             recv_sem=a_recv.at[j], device_id=(leaf, j), device_id_type=MESH,

time: 140 us -> 131 us (0.936)
  Pallas kernels: 136 us -> 127 us
    pallas_call x1, Pallas kernels: 136 us -> 127 us  [per_device(): pl.pallas_call(functools.partial(kernel, n, leaves, xs), out_shape=(jax.S...]
where the time goes in v2:
time: 131 us
  Pallas kernels  127 us (97%)
  local copies, waits for them, and re-layouts  3.65 us (3%)
    pallas_call x1, Pallas kernels, per_device(): pl.pallas_call(functools.partial(kernel, n, leaves, xs), out_shape=(jax.S...  127 us
    unnamed x4, local copies, waits for them, and re-layouts  3.65 us

profile of v2, /device:TPU:0, one launch (start us, length us, event | category | flops | bytes accessed | tf_op | source)
XLA Modules:
  0.0 131.3 jit_solution(11068080545633483715)
XLA Ops:
  0.6 127.0 %shard_map.95 = (bf16[2048,512]{1,0:T(8,128)(2,1)}, f32[16,128]{1,0:T(8,128)}) custom-call(bf16[256,4096]{1,0:T(8,128)(2,1)} %src.1, bf16[512,512]{1,0:T(8,128)(2,1)} %b_ref.1, bf16[64,512]{1,0:T(8,128)(2,1)} %bl_ref.1, bf16[64,512]{1,0:T(8,128)(2,1)} %br_ref.1, bf16[64,512]{1,0:T(8,128)(2,1)} %ci_ref.1, bf16[64,512]{1,0:T(8,128)(2,1)} %co_ref.1, ...), custom_call_target="tpu_custom_call" | custom-call | tf_op jit(solution)/shard_map/pallas_call | solution.py:398
  127.7 0.0 copy-start
  127.7 3.0 %copy.12 = bf16[2048,512]{1,0:T(8,128)(2,1)} copy(bf16[2048,512]{1,0:T(8,128)(2,1)} %get-tuple-element.8) | data formatting | bytes 4194304
  130.7 0.0 copy-done
  130.7 0.6 copy.13
Async XLA Ops:
  127.7 3.1 %copy-start = (f32[16,128]{1,0:T(8,128)S(1)}, f32[16,128]{1,0:T(8,128)}, u32[]{:S(2)}) copy-start(f32[16,128]{1,0:T(8,128)} %get-tuple-element.5) | copy-start | bytes 24580

commit v3 on v2

--- a/solution.py
+++ b/solution.py
@@ -110,19 +110,17 @@
         pl.when(self.z > 0)(lambda: self.down(self.z, self.zs).wait_send())
 
 
-def kernel(
+def gather_kernel(
     n, leaves, xs,
-    src, b_ref, bl_ref, br_ref, ci_ref, co_ref, shot_ref, cell_ref,
-    sol_ref, grad_ref,
-    src_v, rg, rhs, lg, cg, onehot, zacc, u_ref, t_ref, gpart, gbuf, lbuf,
+    src, b_ref, bl_ref, br_ref, ci_ref, co_ref,
+    rhs, cg, fwd_low, back_low,
+    src_v, rg, lg, zacc, u_ref, t_ref,
     src_sem, own_sem, rz, rx, rr, a_send, a_recv, l_send, l_recv, cz, cx, cr,
-    g_send, g_recv, h_send, h_recv,
 ):
     leaf, node = lax.axis_index("leaf"), lax.axis_index("node")
     zs = n // xs
     k, block = bl_ref.shape
     shots = src.shape[0]
-    total = n * shots
 
     barrier = pltpu.get_barrier_semaphore()
 
@@ -188,16 +186,6 @@
             shot_copy(peer(i, 1)).start()
 
     send_shots(1, 2)
-
-    rows_at = 256
-
-    @pl.loop(0, n)
-    def _(j):
-        @pl.loop(0, total // rows_at)
-        def _(r):
-            at = pl.multiple_of(r * rows_at, rows_at)
-            row = lax.broadcasted_iota(jnp.int32, (rows_at, shots), 0) + at
-            onehot[j, pl.ds(at, rows_at), :] = half(jnp.where(row == shot_ref[j], 1.0, 0.0))
 
     src_copy.wait()
     zacc[...] = dot_rows(src_v[:, columns(node)], rg[node, : 4 * k])
@@ -249,8 +237,8 @@
         t_ref[...]
         + lax.dot_general(s1, bl_ref[...], (((0,), (0,)), ((), ())), preferred_element_type=jnp.float32)
     )
-    fwd_low = jnp.concatenate([br_ref[...], fc], axis=0)
-    back_low = jnp.concatenate([bl_ref[...], bc], axis=0)
+    fwd_low[...] = jnp.concatenate([br_ref[...], fc], axis=0)
+    back_low[...] = jnp.concatenate([bl_ref[...], bc], axis=0)
 
     for i in range(1, leaves):
         j = (leaf + i) % leaves
@@ -290,38 +278,74 @@
     coefs.partners(None)
 
     own_copy.wait()
-    sums = jnp.zeros((1, block), jnp.float32)
-
-    def shot_block(j, sums, first):
-        low = cg[j]
-        fwd = half(dot(rhs[j], b_ref[...]) + dot(low[:, : 2 * k], fwd_low))
-        sol = half(dot_rows(fwd, b_ref[...]) + dot(low[:, 2 * k :], back_low))
-
-        @pl.loop(0, total // rows_at)
-        def _(r):
-            rows = pl.ds(pl.multiple_of(r * rows_at, rows_at), rows_at)
-            part = half(dot(onehot[j, rows, :], sol))
-            if first:
-                sol_ref[rows, :] = part
-            else:
-                sol_ref[rows, :] += part
-
-        return sums + jnp.sum(
-            sol.astype(jnp.float32) * fwd.astype(jnp.float32), axis=0, keepdims=True
-        )
-
-    sums = shot_block(node, sums, True)
-
-    def later(i, sums):
+
+    @pl.loop(1, n)
+    def _(i):
         j = peer(i, -1)
         pltpu.make_async_remote_copy(
             src_ref=rhs.at[j], dst_ref=rhs.at[j], send_sem=a_send.at[j],
             recv_sem=a_recv.at[j], device_id=(leaf, j), device_id_type=MESH,
         ).wait_recv()
-        return shot_block(j, sums, False)
-
-    sums = lax.fori_loop(1, n, later, sums)
-    corr = sums / jnp.sqrt(jnp.float32(total))
+
+    basis.finish()
+    coefs.finish()
+    for i in range(1, leaves):
+        leaf_copy(i).wait_send()
+
+    @pl.loop(1, n)
+    def _(i):
+        shot_copy((node + i) % n).wait_send()
+
+
+def sweep_kernel(
+    rhs, low, b_ref, fwd_low, back_low, shot_ref, sol_ref, corr_ref, sol, bt, sums
+):
+    n, shots, block = rhs.shape
+    k2 = fwd_low.shape[0]
+    total = n * shots
+    step = pl.program_id(0)
+
+    @pl.when(step == 0)
+    def _():
+        bt[...] = b_ref[...].T
+        sums[...] = jnp.zeros_like(sums)
+
+        @pl.loop(0, n)
+        def _(j):
+            c = low[j]
+            fwd = half(dot(rhs[j], b_ref[...]) + dot(c[:, :k2], fwd_low[...]))
+            back = half(dot(fwd, bt[...]) + dot(c[:, k2:], back_low[...]))
+            sol[pl.ds(pl.multiple_of(j * shots, shots), shots), :] = back
+            sums[...] += jnp.sum(
+                back.astype(jnp.float32) * fwd.astype(jnp.float32), axis=0, keepdims=True
+            )
+        corr_ref[...] = sums[...] / jnp.sqrt(jnp.float32(total))
+
+    rows = sol_ref.shape[0]
+    row = lax.broadcasted_iota(jnp.int32, (rows, total), 0) + step * rows
+    hit = half(jnp.where(row == shot_ref[...], 1.0, 0.0))
+    sol_ref[...] = half(dot(hit, sol[...]))
+
+
+def gradient_kernel(
+    n, leaves, corr_ref, cell_ref, grad_ref, gpart, gbuf, lbuf, g_send, g_recv, h_send, h_recv
+):
+    leaf, node = lax.axis_index("leaf"), lax.axis_index("node")
+    block = corr_ref.shape[1]
+    corr = corr_ref[...]
+    barrier = pltpu.get_barrier_semaphore()
+
+    @pl.loop(1, n)
+    def _(i):
+        pl.semaphore_signal(
+            barrier, inc=1, device_id=(leaf, (node + i) % n), device_id_type=MESH
+        )
+
+    @pl.loop(1, leaves)
+    def _(i):
+        pl.semaphore_signal(
+            barrier, inc=1, device_id=((leaf + i) % leaves, node), device_id_type=MESH
+        )
 
     cell = cell_ref[...]
     slab = gpart.shape[1]
@@ -335,6 +359,7 @@
         precision=lax.Precision.HIGHEST,
     )
     gpart[...] = placed.reshape(gpart.shape)
+    pl.semaphore_wait(barrier, n - 1 + leaves - 1)
 
     def slab_copy(j, frm):
         return pltpu.make_async_remote_copy(
@@ -372,17 +397,12 @@
         acc = acc + lbuf[g]
     grad_ref[...] = acc
 
-    basis.finish()
-    coefs.finish()
-    for i in range(1, leaves):
-        leaf_copy(i).wait_send()
+    for i in range(1, leaves):
         grad_copy(i, leaf).wait_send()
 
     @pl.loop(1, n)
     def _(i):
-        j = (node + i) % n
-        shot_copy(j).wait_send()
-        slab_copy(j, node).wait_send()
+        slab_copy((node + i) % n, node).wait_send()
 
 
 def per_device(n, leaves, sources, block_inverse, basis_left, basis_right, couple_in, couple_out, column_of_shot, cell_map):
@@ -395,42 +415,72 @@
     bf16, f32 = jnp.bfloat16, jnp.float32
     dma = pltpu.SemaphoreType.DMA
     vmem = pl.BlockSpec(memory_space=pltpu.VMEM)
-    solution_out, grad = pl.pallas_call(
-        functools.partial(kernel, n, leaves, xs),
+    rhs, low, fwd_low, back_low = pl.pallas_call(
+        functools.partial(gather_kernel, n, leaves, xs),
         out_shape=(
-            jax.ShapeDtypeStruct((total, block), bf16),
-            jax.ShapeDtypeStruct((slab, LANES), f32),
+            jax.ShapeDtypeStruct((n, shots, block), bf16),
+            jax.ShapeDtypeStruct((n, shots, 4 * k), bf16),
+            jax.ShapeDtypeStruct((2 * k, block), bf16),
+            jax.ShapeDtypeStruct((2 * k, block), bf16),
         ),
-        in_specs=[pl.BlockSpec(memory_space=pl.ANY)] + [vmem] * 7,
-        out_specs=(vmem, vmem),
+        in_specs=[pl.BlockSpec(memory_space=pl.ANY)] + [vmem] * 5,
+        out_specs=(pl.BlockSpec(memory_space=pl.ANY), vmem, vmem, vmem),
         scratch_shapes=[
             pltpu.VMEM(sources.shape, bf16),
             pltpu.VMEM((n, 5 * k, block), bf16),
-            pltpu.VMEM((n, shots, block), bf16),
             pltpu.VMEM((leaves, shots + k, 2 * k), bf16),
-            pltpu.VMEM((n, shots, 4 * k), bf16),
-            pltpu.VMEM((n, total, shots), bf16),
             pltpu.VMEM((shots, 4 * k), f32),
             pltpu.VMEM((k, block), f32),
             pltpu.VMEM((k, block), f32),
-            pltpu.VMEM((n, slab, LANES), f32),
-            pltpu.VMEM((n, slab, LANES), f32),
-            pltpu.VMEM((leaves, slab, LANES), f32),
             dma, dma,
             dma((zs + 1,)), dma((max(zs * (xs - 1), 1),)), dma((n,)),
             dma((n,)), dma((n,)),
             dma((leaves,)), dma((leaves,)),
             dma((zs + 1,)), dma((max(zs * (xs - 1), 1),)), dma((n,)),
+        ],
+        compiler_params=pltpu.CompilerParams(
+            collective_id=0, has_side_effects=True, vmem_limit_bytes=48 * 1024 * 1024
+        ),
+    )(sources, block_inverse, basis_left, basis_right, couple_in, couple_out)
+
+    rows = min(256, total)
+    whole = lambda *dims: pl.BlockSpec(dims, lambda r: (0,) * len(dims))
+    solution_out, corr = pl.pallas_call(
+        sweep_kernel,
+        grid=(total // rows,),
+        out_shape=(
+            jax.ShapeDtypeStruct((total, block), bf16),
+            jax.ShapeDtypeStruct((1, block), f32),
+        ),
+        in_specs=[
+            whole(n, shots, block), whole(n, shots, 4 * k), whole(block, block),
+            whole(2 * k, block), whole(2 * k, block), whole(1, total),
+        ],
+        out_specs=(pl.BlockSpec((rows, block), lambda r: (r, 0)), whole(1, block)),
+        scratch_shapes=[
+            pltpu.VMEM((total, block), bf16),
+            pltpu.VMEM((block, block), bf16),
+            pltpu.VMEM((1, block), f32),
+        ],
+        compiler_params=pltpu.CompilerParams(vmem_limit_bytes=48 * 1024 * 1024),
+    )(rhs, low, block_inverse, fwd_low, back_low, column_of_shot.reshape(1, -1))
+
+    grad = pl.pallas_call(
+        functools.partial(gradient_kernel, n, leaves),
+        out_shape=jax.ShapeDtypeStruct((slab, LANES), f32),
+        in_specs=[vmem] * 2,
+        out_specs=vmem,
+        scratch_shapes=[
+            pltpu.VMEM((n, slab, LANES), f32),
+            pltpu.VMEM((n, slab, LANES), f32),
+            pltpu.VMEM((leaves, slab, LANES), f32),
             dma((n,)), dma((n,)),
             dma((leaves,)), dma((leaves,)),
         ],
         compiler_params=pltpu.CompilerParams(
-            collective_id=0, has_side_effects=True, vmem_limit_bytes=56 * 1024 * 1024
+            collective_id=1, has_side_effects=True, vmem_limit_bytes=16 * 1024 * 1024
         ),
-    )(
-        sources, block_inverse, basis_left, basis_right, couple_in, couple_out,
-        column_of_shot.reshape(n, 1, shots), cell_map.reshape(1, -1),
-    )
+    )(corr, cell_map.reshape(1, -1))
     return solution_out, grad.reshape(-1)
 
 

time: 131 us -> 129 us (0.985)
  Pallas kernels: 127 us -> 123 us
  local copies, waits for them, and re-layouts: 3.65 us -> 5 us
    pallas_call x1 -> x3, Pallas kernels: 127 us -> 123 us  [the longest x1 100 us: per_device(): pl.pallas_call(functools.partial(gather_kernel, n, leaves, xs), out_shape...]
    unnamed x4 -> x15, local copies, waits for them, and re-layouts: 3.65 us -> 5 us
where the time goes in v3:
time: 129 us; the launch traced here: 128 us
  Pallas kernels  123 us (95%)
  local copies, waits for them, and re-layouts  5 us (4%)
    pallas_call x1, Pallas kernels, per_device(): pl.pallas_call(functools.partial(gather_kernel, n, leaves, xs), out_shape...  100 us
    pallas_call x1, Pallas kernels, per_device(): pl.pallas_call(sweep_kernel, grid=(total // rows,), out_shape=(jax.ShapeD...  11.4 us
    pallas_call x1, Pallas kernels, per_device(): pl.pallas_call(functools.partial(gradient_kernel, n, leaves), out_shape=j...  11 us
    unnamed x15, local copies, waits for them, and re-layouts  5 us

profile of v3, /device:TPU:0, one launch (start us, length us, event | category | flops | bytes accessed | tf_op | source)
XLA Modules:
  0.0 128.3 jit_solution(4499283392469075991)
XLA Ops:
  0.6 0.0 copy-start
  0.6 1.0 copy-done
  1.7 0.0 copy-start.1
  1.7 0.8 copy-done.1
  2.5 0.0 copy-start.2
  2.5 0.8 copy-done.2
  3.4 0.0 copy-start.3
  3.4 0.8 copy-done.3
  4.2 0.0 copy-start.4
  4.2 0.8 copy-done.4
  5.0 0.0 copy-start.5
  5.0 100.3 %shard_map.95 = (bf16[8,256,512]{2,1,0:T(8,128)(2,1)S(1)}, bf16[8,256,256]{2,1,0:T(8,128)(2,1)S(1)}, bf16[128,512]{1,0:T(8,128)(2,1)S(1)}, bf16[128,512]{1,0:T(8,128)(2,1)S(1)}) custom-call(bf16[256,4096]{1,0:T(8,128)(2,1)} %src.1, bf16[512,512]{1,0:T(8,128)(2,1)S(1)} %copy-done, bf16[64,512]{1,0:T(8,128)(2,1)S(1)} %copy-done.1, ...), custom_call_target="tpu_custom_call" | custom-call | tf_op jit(solution)/shard_map/pallas_call | solution.py:418
  105.3 0.0 copy-start.6
  105.3 0.0 copy-done.5
  105.3 11.4 %shard_map.96 = (bf16[2048,512]{1,0:T(8,128)(2,1)}, f32[1,512]{1,0:T(1,128)S(1)}) custom-call(bf16[8,256,512]{2,1,0:T(8,128)(2,1)S(1)} %get-tuple-element.8.rhs, bf16[8,256,256]{2,1,0:T(8,128)(2,1)S(1)} %get-tuple-element.9.low, bf16[512,512]{1,0:T(8,128)(2,1)S(1)} %copy-done, bf16[128,512]{1,0:T(8,128)(2,1)S(1)} %get-tuple-element.10.fwd_low, ...), custom_call_target="tpu_custom_call" | custom-call | tf_op jit(solution)/shard_map/pallas_call | solution.py:448
  116.8 0.0 copy-done.6
  116.8 11.0 %shard_map.97 = f32[16,128]{1,0:T(8,128)S(1)} custom-call(f32[1,512]{1,0:T(1,128)S(1)} %get-tuple-element.13.corr_ref, s32[1,512]{1,0:T(1,128)S(1)} %bitcast.5), custom_call_target="tpu_custom_call" | custom-call | tf_op jit(solution)/shard_map/pallas_call | solution.py:468
  127.7 0.6 copy.11
Async XLA Ops:
  0.6 1.0 copy-start
  1.7 0.8 copy-start.1
  2.5 0.8 copy-start.2
  3.4 0.8 copy-start.3
  4.2 0.8 copy-start.4
  5.0 100.3 %copy-start.5 = (s32[2048]{0:T(1024)S(1)}, s32[2048]{0:T(1024)}, u32[]{:S(2)}) copy-start(s32[2048]{0:T(1024)} %param.14) | copy-start | bytes 24580
  105.3 11.4 %copy-start.6 = (s32[512]{0:T(512)S(1)}, s32[512]{0:T(512)}, u32[]{:S(2)}) copy-start(s32[512]{0:T(512)} %param.15) | copy-start | bytes 6148

commit v4 on v1

--- a/solution.py
+++ b/solution.py
@@ -41,7 +41,7 @@
         )
 
     def slot(self, zz):
-        return zz * self.xs + self.x
+        return zz if self.xsend is None else zz * self.xs + self.x
 
     def up(self, zz, sem):
         return self.copy(self.slot(zz), (self.z + 1) * self.xs + self.x, self.zsend.at[sem])
@@ -50,6 +50,8 @@
         return self.copy(self.slot(zz), (self.z - 1) * self.xs + self.x, self.zsend.at[sem])
 
     def across(self, zz):
+        if self.xsend is None:
+            return []
         return [
             self.copy(
                 self.slot(zz),
@@ -112,17 +114,26 @@
 
 def kernel(
     n, leaves, xs,
-    src, b_ref, bl_ref, br_ref, ci_ref, co_ref, shot_ref, cell_ref,
+    src, b_hbm, bl_hbm, br_hbm, ci_hbm, co_hbm, shot_ref, cell_ref,
     sol_ref, grad_ref,
-    src_v, rg, rhs, lg, cg, onehot, zacc, u_ref, t_ref, gpart, gbuf, lbuf,
-    src_sem, own_sem, rz, rx, rr, a_send, a_recv, l_send, l_recv, cz, cx, cr,
-    g_send, g_recv, h_send, h_recv,
+    b_ref, bl_ref, br_ref, ci_ref, co_ref, bt, col, buf, rg, zpart, zbuf, lg, cg,
+    fwd_low, back_low, onehot, sols, zacc, u_ref, t_ref, sums, gpart, gbuf, lbuf,
+    in_sem, col_sem, rz, rr, x_send, o_send, f_send, a_recv, z_send, z_recv,
+    l_send, l_recv, cz, cx, cr, g_send, g_recv, h_send, h_recv,
 ):
     leaf, node = lax.axis_index("leaf"), lax.axis_index("node")
     zs = n // xs
+    z_at, x_at = node // xs, node % xs
     k, block = bl_ref.shape
     shots = src.shape[0]
     total = n * shots
+
+    pairs = (
+        (b_hbm, b_ref), (bl_hbm, bl_ref), (br_hbm, br_ref), (ci_hbm, ci_ref), (co_hbm, co_ref),
+    )
+    loads = [pltpu.make_async_copy(a, v, in_sem.at[i]) for i, (a, v) in enumerate(pairs)]
+    for c in loads:
+        c.start()
 
     barrier = pltpu.get_barrier_semaphore()
 
@@ -138,15 +149,57 @@
             barrier, inc=1, device_id=((leaf + i) % leaves, node), device_id_type=MESH
         )
 
-    src_copy = pltpu.make_async_copy(src, src_v, src_sem)
-    src_copy.start()
-
     def columns(j):
         return pl.ds(pl.multiple_of(j * block, block), block)
 
-    own_copy = pltpu.make_async_copy(src.at[:, columns(node)], rhs.at[node], own_sem)
-    own_copy.start()
-
+    def column_copy(zz):
+        return pltpu.make_async_copy(
+            src.at[:, columns(zz * xs + x_at)], col.at[zz], col_sem.at[zz]
+        )
+
+    for zz in range(zs):
+        column_copy(zz).start()
+
+    def send(a, slot, sem, dst):
+        return pltpu.make_async_remote_copy(
+            src_ref=a, dst_ref=buf.at[slot], send_sem=sem, recv_sem=a_recv.at[slot],
+            device_id=(leaf, dst), device_id_type=MESH,
+        )
+
+    def arrived(slot):
+        send(buf.at[slot], slot, f_send.at[0], node).wait_recv()
+
+    def passing(x, zz):
+        return jnp.where(zz == z_at, z_at * xs + x, n + x * zs + zz)
+
+    def over_x(i, d):
+        x, zz = (x_at + i) % xs, (z_at + d) % zs
+        return send(
+            src.at[:, columns(zz * xs + x)], passing(x_at, zz),
+            x_send.at[(i - 1) * zs + d], z_at * xs + x,
+        )
+
+    def own_over_z(d):
+        dst = ((z_at + d) % zs) * xs + x_at
+        return send(src.at[:, columns(dst)], node, o_send.at[d], dst)
+
+    def onward(i, d):
+        x, zz = (x_at + i) % xs, (z_at + d) % zs
+        slot = passing(x, zz)
+        return send(buf.at[slot], z_at * xs + x, f_send.at[(i - 1) * zs + d], zz * xs + x_at)
+
+    pl.semaphore_wait(barrier, n - 1 + leaves - 1)
+
+    for i in range(1, xs):
+        @pl.loop(1, zs + 1)
+        def _(d):
+            over_x(i, d % zs).start()
+
+    if zs > 1:
+        own_over_z(1).start()
+
+    for c in loads:
+        c.wait()
     b = b_ref[...]
     u = dot(ci_ref[...], b)
     u_ref[...] = u
@@ -154,58 +207,76 @@
     t = dot_rows(stacked, b)
     t_ref[...] = t[:k]
     v = jnp.concatenate([bl_ref[...], half(t)], axis=0)
-    rg[node, : 4 * k] = v
-    rg[node, 4 * k :, : 4 * k] = half(dot_rows(ci_ref[...], v))
-    rg[node, 4 * k :, 4 * k : 8 * k] = half(
+    rg[z_at, : 4 * k] = v
+    rg[z_at, 4 * k :, : 4 * k] = half(dot_rows(ci_ref[...], v))
+    rg[z_at, 4 * k :, 4 * k : 8 * k] = half(
         dot_rows(br_ref[...], jnp.concatenate([bl_ref[...], stacked], axis=0))
     )
-
-    pl.semaphore_wait(barrier, n - 1 + leaves - 1)
-
-    basis = Tree(rg, rz, rx, rr, leaf, node, zs, xs)
+    basis = Tree(rg, rz, None, rr, leaf, node, zs, xs)
     basis.start()
 
-    def shot_copy(j):
-        return pltpu.make_async_remote_copy(
-            src_ref=src.at[:, columns(j)],
-            dst_ref=rhs.at[node],
-            send_sem=a_send.at[j],
-            recv_sem=a_recv.at[node],
-            device_id=(leaf, j),
-            device_id_type=MESH,
-        )
-
-    @pl.loop(1, n)
-    def _(i):
-        shot_copy((node + i) % n).start()
-
-    rows_at = 256
-
-    @pl.loop(0, n)
-    def _(j):
-        @pl.loop(0, total // rows_at)
-        def _(r):
-            at = pl.multiple_of(r * rows_at, rows_at)
-            row = lax.broadcasted_iota(jnp.int32, (rows_at, shots), 0) + at
-            onehot[j, pl.ds(at, rows_at), :] = half(jnp.where(row == shot_ref[j], 1.0, 0.0))
-
-    src_copy.wait()
-    zacc[...] = dot_rows(src_v[:, columns(node)], rg[node, : 4 * k])
-
-    def project(slot):
-        zacc[...] += dot_rows(src_v[:, columns(slot)], rg[slot, : 4 * k])
+    bt[...] = b.T
+
+    rows_at = min(256, total)
+
+    @pl.loop(0, total // rows_at)
+    def _(r):
+        at = pl.multiple_of(r * rows_at, rows_at)
+        row = lax.broadcasted_iota(jnp.int32, (rows_at, total), 0) + at
+        onehot[pl.ds(at, rows_at), :] = half(jnp.where(row == shot_ref[...], 1.0, 0.0))
+
+    for zz in range(zs):
+        column_copy(zz).wait()
+    zacc[...] = dot_rows(col[z_at], rg[z_at, : 4 * k])
+
+    def project(zz):
+        zacc[...] += dot_rows(col[zz], rg[zz, : 4 * k])
 
     for hop in range(1, zs):
         basis.relay(hop, project)
-    basis.partners(project)
-
-    s = rg[0, 4 * k :, :].astype(jnp.float32)
-    for j in range(1, n):
-        s = s + rg[j, 4 * k :, :].astype(jnp.float32)
-    s3t = half(s[:, :k])
-    ss = half(s[:, 4 * k : 8 * k])
-    f = s[:, : 4 * k] + dot(s3t, ss)
+        if hop + 1 < zs:
+            own_over_z(hop + 1).start()
+
+    late = max(zs - zs // 3, 1)
+    for i in range(1, xs):
+        @pl.loop(1, zs)
+        def _(d):
+            arrived(passing((x_at + i) % xs, (z_at + d) % zs))
+            pl.when(d < late)(lambda: onward(i, d).start())
+        arrived(passing((x_at + i) % xs, z_at))
+
+    s_part = rg[0, 4 * k :, :].astype(jnp.float32)
+    for j in range(1, zs):
+        s_part = s_part + rg[j, 4 * k :, :].astype(jnp.float32)
+
+    def partial_copy(i, frm):
+        return pltpu.make_async_remote_copy(
+            src_ref=zpart.at[i - 1], dst_ref=zbuf.at[frm], send_sem=z_send.at[i],
+            recv_sem=z_recv.at[frm], device_id=(leaf, z_at * xs + (x_at + i) % xs),
+            device_id_type=MESH,
+        )
+
+    for i in range(1, xs):
+        x = (x_at + i) % xs
+        acc = jnp.zeros((shots, 4 * k), jnp.float32)
+        for zz in range(zs):
+            acc = acc + dot_rows(buf[passing(x, zz)], rg[zz, : 4 * k])
+        zpart[i - 1, :shots] = half(acc)
+        zpart[i - 1, shots : shots + k] = half(s_part[:, : 4 * k])
+        zpart[i - 1, shots + k :] = half(s_part[:, 4 * k : 8 * k])
+        partial_copy(i, x_at).start()
     z = zacc[...]
+    left, right = s_part[:, : 4 * k], s_part[:, 4 * k : 8 * k]
+    for i in range(1, xs):
+        x = (x_at + i) % xs
+        partial_copy(i, x).wait_recv()
+        z = z + zbuf[x, :shots].astype(jnp.float32)
+        left = left + zbuf[x, shots : shots + k].astype(jnp.float32)
+        right = right + zbuf[x, shots + k :].astype(jnp.float32)
+
+    s3t = half(left[:, :k])
+    ss = half(right)
+    f = left + dot(s3t, ss)
     proj = half(z[:, :k])
     zf = z + dot(proj, ss)
     carry, z2, z3 = zf[:, k : 2 * k], zf[:, 2 * k : 3 * k], zf[:, 3 * k :]
@@ -215,34 +286,27 @@
     lg[leaf, :shots] = half(jnp.concatenate([carry, lift], axis=1))
     lg[leaf, shots:] = half(-jnp.concatenate([f[:, k : 2 * k], lift_map], axis=1))
 
-    def leaf_copy(i):
+    def leaf_copy(i, frm):
         return pltpu.make_async_remote_copy(
-            src_ref=lg.at[leaf],
-            dst_ref=lg.at[leaf],
-            send_sem=l_send.at[i],
-            recv_sem=l_recv.at[leaf],
-            device_id=((leaf + i) % leaves, node),
+            src_ref=lg.at[leaf], dst_ref=lg.at[frm], send_sem=l_send.at[i],
+            recv_sem=l_recv.at[frm], device_id=((leaf + i) % leaves, node),
             device_id_type=MESH,
         )
 
     for i in range(1, leaves):
-        leaf_copy(i).start()
+        leaf_copy(i, leaf).start()
 
     fc = half(u_ref[...] + dot(s3t, br_ref[...]))
-    s1 = half(s[:, 5 * k : 6 * k])
+    s1 = half(right[:, k : 2 * k])
     bc = half(
         t_ref[...]
         + lax.dot_general(s1, bl_ref[...], (((0,), (0,)), ((), ())), preferred_element_type=jnp.float32)
     )
-    fwd_low = jnp.concatenate([br_ref[...], fc], axis=0)
-    back_low = jnp.concatenate([bl_ref[...], bc], axis=0)
+    fwd_low[...] = jnp.concatenate([br_ref[...], fc], axis=0)
+    back_low[...] = jnp.concatenate([bl_ref[...], bc], axis=0)
 
     for i in range(1, leaves):
-        j = (leaf + i) % leaves
-        pltpu.make_async_remote_copy(
-            src_ref=lg.at[leaf], dst_ref=lg.at[j], send_sem=l_send.at[0],
-            recv_sem=l_recv.at[j], device_id=(j, node), device_id_type=MESH,
-        ).wait_recv()
+        leaf_copy(i, (leaf + i) % leaves).wait_recv()
 
     incoming = jnp.zeros((shots, k), jnp.float32)
     own_in = jnp.zeros((shots, k), jnp.float32)
@@ -271,41 +335,36 @@
     coefs.start()
     for hop in range(1, zs):
         coefs.relay(hop, None)
+        if hop == 1:
+            for i in range(1, xs):
+                @pl.loop(late, zs)
+                def _(d):
+                    onward(i, d).start()
     coefs.partners(None)
 
-    own_copy.wait()
-    sums = jnp.zeros((1, block), jnp.float32)
-
-    def shot_block(j, sums, first):
+    sums[...] = jnp.zeros_like(sums)
+
+    def shot_block(j, rhs):
         low = cg[j]
-        fwd = half(dot(rhs[j], b_ref[...]) + dot(low[:, : 2 * k], fwd_low))
-        sol = half(dot_rows(fwd, b_ref[...]) + dot(low[:, 2 * k :], back_low))
-
-        @pl.loop(0, total // rows_at)
-        def _(r):
-            rows = pl.ds(pl.multiple_of(r * rows_at, rows_at), rows_at)
-            part = half(dot(onehot[j, rows, :], sol))
-            if first:
-                sol_ref[rows, :] = part
-            else:
-                sol_ref[rows, :] += part
-
-        return sums + jnp.sum(
+        fwd = half(dot(rhs, b_ref[...]) + dot(low[:, : 2 * k], fwd_low[...]))
+        sol = half(dot(fwd, bt[...]) + dot(low[:, 2 * k :], back_low[...]))
+        sols[pl.ds(pl.multiple_of(j * shots, shots), shots), :] = sol
+        sums[...] += jnp.sum(
             sol.astype(jnp.float32) * fwd.astype(jnp.float32), axis=0, keepdims=True
         )
 
-    sums = shot_block(node, sums, True)
-
-    def later(i, sums):
-        j = (node + n - i) % n
-        pltpu.make_async_remote_copy(
-            src_ref=rhs.at[j], dst_ref=rhs.at[j], send_sem=a_send.at[j],
-            recv_sem=a_recv.at[j], device_id=(leaf, j), device_id_type=MESH,
-        ).wait_recv()
-        return shot_block(j, sums, False)
-
-    sums = lax.fori_loop(1, n, later, sums)
-    corr = sums / jnp.sqrt(jnp.float32(total))
+    shot_block(node, col[z_at])
+    for i in range(1, xs):
+        j = z_at * xs + (x_at + i) % xs
+        shot_block(j, buf[j])
+    for i in range(xs):
+        @pl.loop(1, zs)
+        def _(d):
+            j = ((z_at + zs - d) % zs) * xs + (x_at + i) % xs
+            arrived(j)
+            shot_block(j, buf[j])
+
+    corr = sums[...] / jnp.sqrt(jnp.float32(total))
 
     cell = cell_ref[...]
     slab = gpart.shape[1]
@@ -330,6 +389,15 @@
     def _(i):
         slab_copy((node + i) % n, node).start()
 
+    def permute(first, last):
+        @pl.loop(first, last)
+        def _(r):
+            rows = pl.ds(pl.multiple_of(r * rows_at, rows_at), rows_at)
+            sol_ref[rows, :] = half(dot(onehot[rows, :], sols[...]))
+
+    steps = total // rows_at
+    permute(0, steps // 2)
+
     own = gpart[node]
 
     def add_slab(i, acc):
@@ -349,6 +417,7 @@
 
     for i in range(1, leaves):
         grad_copy(i, leaf).start()
+    permute(steps // 2, steps)
     for i in range(1, leaves):
         grad_copy(i, (leaf + leaves - i) % leaves).wait_recv()
     acc = lbuf[0]
@@ -356,17 +425,27 @@
         acc = acc + lbuf[g]
     grad_ref[...] = acc
 
+
     basis.finish()
     coefs.finish()
     for i in range(1, leaves):
-        leaf_copy(i).wait_send()
+        leaf_copy(i, leaf).wait_send()
         grad_copy(i, leaf).wait_send()
+    for i in range(1, xs):
+        partial_copy(i, x_at).wait_send()
+
+        @pl.loop(0, zs)
+        def _(d):
+            over_x(i, d).wait_send()
+            pl.when(d > 0)(lambda: onward(i, d).wait_send())
+
+    @pl.loop(1, zs)
+    def _(d):
+        own_over_z(d).wait_send()
 
     @pl.loop(1, n)
     def _(i):
-        j = (node + i) % n
-        shot_copy(j).wait_send()
-        slab_copy(j, node).wait_send()
+        slab_copy((node + i) % n, node).wait_send()
 
 
 def per_device(n, leaves, sources, block_inverse, basis_left, basis_right, couple_in, couple_out, column_of_shot, cell_map):
@@ -378,33 +457,45 @@
     slab = CELL_DEV // LANES
     bf16, f32 = jnp.bfloat16, jnp.float32
     dma = pltpu.SemaphoreType.DMA
+    anywhere = pl.BlockSpec(memory_space=pl.ANY)
     vmem = pl.BlockSpec(memory_space=pltpu.VMEM)
+    vectors = max(zs * (xs - 1), 1)
+    small = pltpu.VMEM((k, block), bf16)
     solution_out, grad = pl.pallas_call(
         functools.partial(kernel, n, leaves, xs),
         out_shape=(
             jax.ShapeDtypeStruct((total, block), bf16),
             jax.ShapeDtypeStruct((slab, LANES), f32),
         ),
-        in_specs=[pl.BlockSpec(memory_space=pl.ANY)] + [vmem] * 7,
+        in_specs=[anywhere] * 6 + [vmem] * 2,
         out_specs=(vmem, vmem),
         scratch_shapes=[
-            pltpu.VMEM(sources.shape, bf16),
-            pltpu.VMEM((n, 5 * k, block), bf16),
-            pltpu.VMEM((n, shots, block), bf16),
+            pltpu.VMEM((block, block), bf16), small, small, small, small,
+            pltpu.VMEM((block, block), bf16),
+            pltpu.VMEM((zs, shots, block), bf16),
+            pltpu.VMEM((2 * n, shots, block), bf16),
+            pltpu.VMEM((zs, 5 * k, block), bf16),
+            pltpu.VMEM((max(xs - 1, 1), shots + 2 * k, 4 * k), bf16),
+            pltpu.VMEM((xs, shots + 2 * k, 4 * k), bf16),
             pltpu.VMEM((leaves, shots + k, 2 * k), bf16),
             pltpu.VMEM((n, shots, 4 * k), bf16),
-            pltpu.VMEM((n, total, shots), bf16),
+            pltpu.VMEM((2 * k, block), bf16),
+            pltpu.VMEM((2 * k, block), bf16),
+            pltpu.VMEM((total, total), bf16),
+            pltpu.VMEM((total, block), bf16),
             pltpu.VMEM((shots, 4 * k), f32),
             pltpu.VMEM((k, block), f32),
             pltpu.VMEM((k, block), f32),
+            pltpu.VMEM((1, block), f32),
             pltpu.VMEM((n, slab, LANES), f32),
             pltpu.VMEM((n, slab, LANES), f32),
             pltpu.VMEM((leaves, slab, LANES), f32),
-            dma, dma,
-            dma((zs + 1,)), dma((max(zs * (xs - 1), 1),)), dma((n,)),
-            dma((n,)), dma((n,)),
+            dma((5,)), dma((zs,)),
+            dma((zs + 1,)), dma((zs,)),
+            dma((vectors,)), dma((zs,)), dma((vectors,)), dma((2 * n,)),
+            dma((xs,)), dma((xs,)),
             dma((leaves,)), dma((leaves,)),
-            dma((zs + 1,)), dma((max(zs * (xs - 1), 1),)), dma((n,)),
+            dma((zs + 1,)), dma((vectors,)), dma((n,)),
             dma((n,)), dma((n,)),
             dma((leaves,)), dma((leaves,)),
         ],
@@ -413,7 +504,7 @@
         ),
     )(
         sources, block_inverse, basis_left, basis_right, couple_in, couple_out,
-        column_of_shot.reshape(n, 1, shots), cell_map.reshape(1, -1),
+        column_of_shot.reshape(1, -1), cell_map.reshape(1, -1),
     )
     return solution_out, grad.reshape(-1)
 

time: 140 us -> 108 us (0.77)
  Pallas kernels: 136 us -> 104 us
    pallas_call x1, Pallas kernels: 136 us -> 104 us  [per_device(): pl.pallas_call(functools.partial(kernel, n, leaves, xs), out_shape=(jax.S...]
where the time goes in v4:
time: 108 us
  Pallas kernels  104 us (96%)
  local copies, waits for them, and re-layouts  3.65 us (3%)
    pallas_call x1, Pallas kernels, per_device(): pl.pallas_call(functools.partial(kernel, n, leaves, xs), out_shape=(jax.S...  104 us
    unnamed x4, local copies, waits for them, and re-layouts  3.65 us

profile of v4, /device:TPU:0, one launch (start us, length us, event | category | flops | bytes accessed | tf_op | source)
XLA Modules:
  0.0 107.8 jit_solution(7928722912001984155)
XLA Ops:
  0.6 103.5 %shard_map.95 = (bf16[2048,512]{1,0:T(8,128)(2,1)}, f32[16,128]{1,0:T(8,128)}) custom-call(bf16[256,4096]{1,0:T(8,128)(2,1)} %src.1, bf16[512,512]{1,0:T(8,128)(2,1)} %b_hbm.1, bf16[64,512]{1,0:T(8,128)(2,1)} %bl_hbm.1, bf16[64,512]{1,0:T(8,128)(2,1)} %br_hbm.1, bf16[64,512]{1,0:T(8,128)(2,1)} %ci_hbm.1, bf16[64,512]{1,0:T(8,128)(2,1)} %co_hbm.1, ...), custom_call_target="tpu_custom_call" | custom-call | tf_op jit(solution)/shard_map/pallas_call | solution.py:464
  104.1 0.0 copy-start
  104.2 3.0 %copy.12 = bf16[2048,512]{1,0:T(8,128)(2,1)} copy(bf16[2048,512]{1,0:T(8,128)(2,1)} %get-tuple-element.8) | data formatting | bytes 4194304
  107.2 0.0 copy-done
  107.2 0.6 copy.13
Async XLA Ops:
  104.1 3.1 %copy-start = (f32[16,128]{1,0:T(8,128)S(1)}, f32[16,128]{1,0:T(8,128)}, u32[]{:S(2)}) copy-start(f32[16,128]{1,0:T(8,128)} %get-tuple-element.5) | copy-start | bytes 24580

commit v5 on v4

--- a/solution.py
+++ b/solution.py
@@ -215,16 +215,6 @@
     basis = Tree(rg, rz, None, rr, leaf, node, zs, xs)
     basis.start()
 
-    bt[...] = b.T
-
-    rows_at = min(256, total)
-
-    @pl.loop(0, total // rows_at)
-    def _(r):
-        at = pl.multiple_of(r * rows_at, rows_at)
-        row = lax.broadcasted_iota(jnp.int32, (rows_at, total), 0) + at
-        onehot[pl.ds(at, rows_at), :] = half(jnp.where(row == shot_ref[...], 1.0, 0.0))
-
     for zz in range(zs):
         column_copy(zz).wait()
     zacc[...] = dot_rows(col[z_at], rg[z_at, : 4 * k])
@@ -234,10 +224,12 @@
 
     for hop in range(1, zs):
         basis.relay(hop, project)
-        if hop + 1 < zs:
-            own_over_z(hop + 1).start()
-
-    late = max(zs - zs // 3, 1)
+        if hop == max(zs - 2, 1):
+            @pl.loop(2, zs)
+            def _(d):
+                own_over_z(d).start()
+
+    late = max(zs // 2, 1)
     for i in range(1, xs):
         @pl.loop(1, zs)
         def _(d):
@@ -265,6 +257,18 @@
         zpart[i - 1, shots : shots + k] = half(s_part[:, : 4 * k])
         zpart[i - 1, shots + k :] = half(s_part[:, 4 * k : 8 * k])
         partial_copy(i, x_at).start()
+
+    rows_at = min(256, total)
+    steps = total // rows_at
+
+    def one_hot(first, last):
+        @pl.loop(first, last)
+        def _(r):
+            at = pl.multiple_of(r * rows_at, rows_at)
+            row = lax.broadcasted_iota(jnp.int32, (rows_at, total), 0) + at
+            onehot[pl.ds(at, rows_at), :] = half(jnp.where(row == shot_ref[...], 1.0, 0.0))
+
+    one_hot(0, steps // 2)
     z = zacc[...]
     left, right = s_part[:, : 4 * k], s_part[:, 4 * k : 8 * k]
     for i in range(1, xs):
@@ -304,6 +308,9 @@
     )
     fwd_low[...] = jnp.concatenate([br_ref[...], fc], axis=0)
     back_low[...] = jnp.concatenate([bl_ref[...], bc], axis=0)
+
+    one_hot(steps // 2, steps)
+    bt[...] = b_ref[...].T
 
     for i in range(1, leaves):
         leaf_copy(i, (leaf + i) % leaves).wait_recv()
@@ -335,7 +342,7 @@
     coefs.start()
     for hop in range(1, zs):
         coefs.relay(hop, None)
-        if hop == 1:
+        if hop == max(zs - 2, 1):
             for i in range(1, xs):
                 @pl.loop(late, zs)
                 def _(d):
@@ -395,7 +402,6 @@
             rows = pl.ds(pl.multiple_of(r * rows_at, rows_at), rows_at)
             sol_ref[rows, :] = half(dot(onehot[rows, :], sols[...]))
 
-    steps = total // rows_at
     permute(0, steps // 2)
 
     own = gpart[node]

time: 108 us -> 105 us (0.972)
  Pallas kernels: 104 us -> 101 us
    pallas_call x1, Pallas kernels: 104 us -> 101 us  [per_device(): pl.pallas_call(functools.partial(kernel, n, leaves, xs), out_shape=(jax.S...]
where the time goes in v5:
time: 105 us
  Pallas kernels  101 us (96%)
  local copies, waits for them, and re-layouts  3.65 us (3%)
    pallas_call x1, Pallas kernels, per_device(): pl.pallas_call(functools.partial(kernel, n, leaves, xs), out_shape=(jax.S...  101 us
    unnamed x4, local copies, waits for them, and re-layouts  3.65 us

profile of v5, /device:TPU:0, one launch (start us, length us, event | category | flops | bytes accessed | tf_op | source)
XLA Modules:
  0.0 105.2 jit_solution(2416949453276278343)
XLA Ops:
  0.6 100.9 %shard_map.95 = (bf16[2048,512]{1,0:T(8,128)(2,1)}, f32[16,128]{1,0:T(8,128)}) custom-call(bf16[256,4096]{1,0:T(8,128)(2,1)} %src.1, bf16[512,512]{1,0:T(8,128)(2,1)} %b_hbm.1, bf16[64,512]{1,0:T(8,128)(2,1)} %bl_hbm.1, bf16[64,512]{1,0:T(8,128)(2,1)} %br_hbm.1, bf16[64,512]{1,0:T(8,128)(2,1)} %ci_hbm.1, bf16[64,512]{1,0:T(8,128)(2,1)} %co_hbm.1, ...), custom_call_target="tpu_custom_call" | custom-call | tf_op jit(solution)/shard_map/pallas_call | solution.py:470
  101.6 0.0 copy-start
  101.6 3.0 %copy.12 = bf16[2048,512]{1,0:T(8,128)(2,1)} copy(bf16[2048,512]{1,0:T(8,128)(2,1)} %get-tuple-element.8) | data formatting | bytes 4194304
  104.6 0.0 copy-done
  104.6 0.6 copy.13
Async XLA Ops:
  101.6 3.1 %copy-start = (f32[16,128]{1,0:T(8,128)S(1)}, f32[16,128]{1,0:T(8,128)}, u32[]{:S(2)}) copy-start(f32[16,128]{1,0:T(8,128)} %get-tuple-element.5) | copy-start | bytes 24580

commit v6 on v5

--- a/solution.py
+++ b/solution.py
@@ -25,15 +25,19 @@
 
 
 class Tree:
-    def __init__(self, buf, zsend, xsend, recv, leaf, node, zs, xs):
+    def __init__(self, buf, part, parts, zsend, xsend, recv, leaf, node, zs, xs):
+        step = buf.shape[1] // parts
+        self.rows = pl.ds(part * step, step)
+        zsend, recv = zsend.at[part], recv.at[part]
+        xsend = None if xsend is None else xsend.at[part]
         self.buf, self.zsend, self.xsend, self.recv = buf, zsend, xsend, recv
         self.leaf, self.zs, self.xs = leaf, zs, xs
         self.z, self.x = node // xs, node % xs
 
     def copy(self, slot, dst, sem):
         return pltpu.make_async_remote_copy(
-            src_ref=self.buf.at[slot],
-            dst_ref=self.buf.at[slot],
+            src_ref=self.buf.at[slot, self.rows],
+            dst_ref=self.buf.at[slot, self.rows],
             send_sem=sem,
             recv_sem=self.recv.at[slot],
             device_id=(self.leaf, dst),
@@ -70,7 +74,7 @@
     def wait_slot(self, slot):
         self.copy(slot, 0, self.zsend.at[0]).wait_recv()
 
-    def relay(self, hop, use):
+    def relay(self, hop):
         below, above = self.z - hop, self.z + hop
 
         @pl.when(below >= 0)
@@ -87,18 +91,12 @@
             for c in self.across(above):
                 c.start()
 
-        if use is not None:
-            pl.when(below >= 0)(lambda: use(self.slot(below)))
-            pl.when(above < self.zs)(lambda: use(self.slot(above)))
-
-    def partners(self, use):
+    def partners(self):
         for i in range(1, self.xs):
             @pl.loop(0, self.zs)
             def _(zz):
                 slot = zz * self.xs + (self.x + i) % self.xs
                 self.wait_slot(slot)
-                if use is not None:
-                    use(slot)
 
     def finish(self):
         @pl.loop(0, self.zs)
@@ -181,22 +179,12 @@
 
     def own_over_z(d):
         dst = ((z_at + d) % zs) * xs + x_at
-        return send(src.at[:, columns(dst)], node, o_send.at[d], dst)
+        return send(col.at[(z_at + d) % zs], node, o_send.at[d], dst)
 
     def onward(i, d):
         x, zz = (x_at + i) % xs, (z_at + d) % zs
         slot = passing(x, zz)
         return send(buf.at[slot], z_at * xs + x, f_send.at[(i - 1) * zs + d], zz * xs + x_at)
-
-    pl.semaphore_wait(barrier, n - 1 + leaves - 1)
-
-    for i in range(1, xs):
-        @pl.loop(1, zs + 1)
-        def _(d):
-            over_x(i, d % zs).start()
-
-    if zs > 1:
-        own_over_z(1).start()
 
     for c in loads:
         c.wait()
@@ -212,29 +200,44 @@
     rg[z_at, 4 * k :, 4 * k : 8 * k] = half(
         dot_rows(br_ref[...], jnp.concatenate([bl_ref[...], stacked], axis=0))
     )
-    basis = Tree(rg, rz, None, rr, leaf, node, zs, xs)
-    basis.start()
+    pl.semaphore_wait(barrier, n - 1 + leaves - 1)
+
+    parts = 2
+    basis = [Tree(rg, p, parts, rz, None, rr, leaf, node, zs, xs) for p in range(parts)]
+    for part in basis:
+        part.start()
+
+    for i in range(1, xs):
+        @pl.loop(1, zs + 1)
+        def _(d):
+            over_x(i, d % zs).start()
 
     for zz in range(zs):
         column_copy(zz).wait()
+    if zs > 1:
+        own_over_z(1).start()
+
     zacc[...] = dot_rows(col[z_at], rg[z_at, : 4 * k])
 
     def project(zz):
         zacc[...] += dot_rows(col[zz], rg[zz, : 4 * k])
 
     for hop in range(1, zs):
-        basis.relay(hop, project)
+        for part in basis:
+            part.relay(hop)
+        pl.when(z_at >= hop)(lambda: project(z_at - hop))
+        pl.when(z_at + hop < zs)(lambda: project(z_at + hop))
         if hop == max(zs - 2, 1):
             @pl.loop(2, zs)
             def _(d):
                 own_over_z(d).start()
 
-    late = max(zs // 2, 1)
+    early, late = 1 + (zs - 1) // 3, 1 + 2 * (zs - 1) // 3
     for i in range(1, xs):
         @pl.loop(1, zs)
         def _(d):
             arrived(passing((x_at + i) % xs, (z_at + d) % zs))
-            pl.when(d < late)(lambda: onward(i, d).start())
+            pl.when(d < early)(lambda: onward(i, d).start())
         arrived(passing((x_at + i) % xs, z_at))
 
     s_part = rg[0, 4 * k :, :].astype(jnp.float32)
@@ -299,6 +302,10 @@
 
     for i in range(1, leaves):
         leaf_copy(i, leaf).start()
+    for i in range(1, xs):
+        @pl.loop(early, late)
+        def _(d):
+            onward(i, d).start()
 
     fc = half(u_ref[...] + dot(s3t, br_ref[...]))
     s1 = half(right[:, k : 2 * k])
@@ -338,16 +345,19 @@
         jnp.concatenate([z[:, :k], -own_in, proj_fwd, -own_ret], axis=1)
     )
 
-    coefs = Tree(cg, cz, cx, cr, leaf, node, zs, xs)
-    coefs.start()
+    coefs = [Tree(cg, p, parts, cz, cx, cr, leaf, node, zs, xs) for p in range(parts)]
+    for part in coefs:
+        part.start()
     for hop in range(1, zs):
-        coefs.relay(hop, None)
+        for part in coefs:
+            part.relay(hop)
         if hop == max(zs - 2, 1):
             for i in range(1, xs):
                 @pl.loop(late, zs)
                 def _(d):
                     onward(i, d).start()
-    coefs.partners(None)
+    for part in coefs:
+        part.partners()
 
     sums[...] = jnp.zeros_like(sums)
 
@@ -432,8 +442,8 @@
     grad_ref[...] = acc
 
 
-    basis.finish()
-    coefs.finish()
+    for part in basis + coefs:
+        part.finish()
     for i in range(1, leaves):
         leaf_copy(i, leaf).wait_send()
         grad_copy(i, leaf).wait_send()
@@ -497,11 +507,11 @@
             pltpu.VMEM((n, slab, LANES), f32),
             pltpu.VMEM((leaves, slab, LANES), f32),
             dma((5,)), dma((zs,)),
-            dma((zs + 1,)), dma((zs,)),
+            dma((2, zs + 1)), dma((2, zs)),
             dma((vectors,)), dma((zs,)), dma((vectors,)), dma((2 * n,)),
             dma((xs,)), dma((xs,)),
             dma((leaves,)), dma((leaves,)),
-            dma((zs + 1,)), dma((vectors,)), dma((n,)),
+            dma((2, zs + 1)), dma((2, vectors)), dma((2, n)),
             dma((n,)), dma((n,)),
             dma((leaves,)), dma((leaves,)),
         ],

time: 105 us -> 99.6 us (0.949)
  Pallas kernels: 101 us -> 95.1 us
    pallas_call x1, Pallas kernels: 101 us -> 95.1 us  [per_device(): pl.pallas_call(functools.partial(kernel, n, leaves, xs), out_shape=(jax.S...]
where the time goes in v6:
time: 99.6 us; the launch traced here: 99.4 us
  Pallas kernels  95.1 us (95%)
  local copies, waits for them, and re-layouts  3.65 us (4%)
    pallas_call x1, Pallas kernels, per_device(): pl.pallas_call(functools.partial(kernel, n, leaves, xs), out_shape=(jax.S...  95.1 us
    unnamed x4, local copies, waits for them, and re-layouts  3.65 us

profile of v6, /device:TPU:0, one launch (start us, length us, event | category | flops | bytes accessed | tf_op | source)
XLA Modules:
  0.0 99.4 jit_solution(7597091397600440477)
XLA Ops:
  0.6 95.1 %shard_map.95 = (bf16[2048,512]{1,0:T(8,128)(2,1)}, f32[16,128]{1,0:T(8,128)}) custom-call(bf16[256,4096]{1,0:T(8,128)(2,1)} %src.1, bf16[512,512]{1,0:T(8,128)(2,1)} %b_hbm.1, bf16[64,512]{1,0:T(8,128)(2,1)} %bl_hbm.1, bf16[64,512]{1,0:T(8,128)(2,1)} %br_hbm.1, bf16[64,512]{1,0:T(8,128)(2,1)} %ci_hbm.1, bf16[64,512]{1,0:T(8,128)(2,1)} %co_hbm.1, ...), custom_call_target="tpu_custom_call" | custom-call | tf_op jit(solution)/shard_map/pallas_call | solution.py:480
  95.7 0.0 copy-start
  95.7 3.0 %copy.12 = bf16[2048,512]{1,0:T(8,128)(2,1)} copy(bf16[2048,512]{1,0:T(8,128)(2,1)} %get-tuple-element.8) | data formatting | bytes 4194304
  98.8 0.0 copy-done
  98.8 0.6 copy.13
Async XLA Ops:
  95.7 3.1 %copy-start = (f32[16,128]{1,0:T(8,128)S(1)}, f32[16,128]{1,0:T(8,128)}, u32[]{:S(2)}) copy-start(f32[16,128]{1,0:T(8,128)} %get-tuple-element.5) | copy-start | bytes 24580

commit v7 on v6

--- a/solution.py
+++ b/solution.py
@@ -202,7 +202,7 @@
     )
     pl.semaphore_wait(barrier, n - 1 + leaves - 1)
 
-    parts = 2
+    parts = rz.shape[0]
     basis = [Tree(rg, p, parts, rz, None, rr, leaf, node, zs, xs) for p in range(parts)]
     for part in basis:
         part.start()
@@ -216,50 +216,6 @@
         column_copy(zz).wait()
     if zs > 1:
         own_over_z(1).start()
-
-    zacc[...] = dot_rows(col[z_at], rg[z_at, : 4 * k])
-
-    def project(zz):
-        zacc[...] += dot_rows(col[zz], rg[zz, : 4 * k])
-
-    for hop in range(1, zs):
-        for part in basis:
-            part.relay(hop)
-        pl.when(z_at >= hop)(lambda: project(z_at - hop))
-        pl.when(z_at + hop < zs)(lambda: project(z_at + hop))
-        if hop == max(zs - 2, 1):
-            @pl.loop(2, zs)
-            def _(d):
-                own_over_z(d).start()
-
-    early, late = 1 + (zs - 1) // 3, 1 + 2 * (zs - 1) // 3
-    for i in range(1, xs):
-        @pl.loop(1, zs)
-        def _(d):
-            arrived(passing((x_at + i) % xs, (z_at + d) % zs))
-            pl.when(d < early)(lambda: onward(i, d).start())
-        arrived(passing((x_at + i) % xs, z_at))
-
-    s_part = rg[0, 4 * k :, :].astype(jnp.float32)
-    for j in range(1, zs):
-        s_part = s_part + rg[j, 4 * k :, :].astype(jnp.float32)
-
-    def partial_copy(i, frm):
-        return pltpu.make_async_remote_copy(
-            src_ref=zpart.at[i - 1], dst_ref=zbuf.at[frm], send_sem=z_send.at[i],
-            recv_sem=z_recv.at[frm], device_id=(leaf, z_at * xs + (x_at + i) % xs),
-            device_id_type=MESH,
-        )
-
-    for i in range(1, xs):
-        x = (x_at + i) % xs
-        acc = jnp.zeros((shots, 4 * k), jnp.float32)
-        for zz in range(zs):
-            acc = acc + dot_rows(buf[passing(x, zz)], rg[zz, : 4 * k])
-        zpart[i - 1, :shots] = half(acc)
-        zpart[i - 1, shots : shots + k] = half(s_part[:, : 4 * k])
-        zpart[i - 1, shots + k :] = half(s_part[:, 4 * k : 8 * k])
-        partial_copy(i, x_at).start()
 
     rows_at = min(256, total)
     steps = total // rows_at
@@ -272,26 +228,75 @@
             onehot[pl.ds(at, rows_at), :] = half(jnp.where(row == shot_ref[...], 1.0, 0.0))
 
     one_hot(0, steps // 2)
-    z = zacc[...]
+    bt[...] = b.T
+
+    for hop in range(1, zs):
+        for part in basis:
+            part.relay(hop)
+        if hop == max(zs - 2, 1):
+            @pl.loop(2, zs)
+            def _(d):
+                own_over_z(d).start()
+
+    early, late = 1 + (zs - 1) // 3, 1 + 2 * (zs - 1) // 3
+    for i in range(1, xs):
+        @pl.loop(1, zs)
+        def _(d):
+            arrived(passing((x_at + i) % xs, (z_at + d) % zs))
+            pl.when(d < early)(lambda: onward(i, d).start())
+        arrived(passing((x_at + i) % xs, z_at))
+
+    s_part = rg[0, 4 * k :, :].astype(jnp.float32)
+    for j in range(1, zs):
+        s_part = s_part + rg[j, 4 * k :, :].astype(jnp.float32)
+
+    def partial_copy(i, frm, rows, sem):
+        return pltpu.make_async_remote_copy(
+            src_ref=zpart.at[i - 1, rows], dst_ref=zbuf.at[frm, rows],
+            send_sem=z_send.at[sem, i], recv_sem=z_recv.at[sem, frm],
+            device_id=(leaf, z_at * xs + (x_at + i) % xs), device_id_type=MESH,
+        )
+
+    grams, projections = pl.ds(shots, 2 * k), pl.ds(0, shots)
+    for i in range(1, xs):
+        zpart[i - 1, shots : shots + k] = half(s_part[:, : 4 * k])
+        zpart[i - 1, shots + k :] = half(s_part[:, 4 * k : 8 * k])
+        partial_copy(i, x_at, grams, 0).start()
+    for i in range(1, xs):
+        x = (x_at + i) % xs
+        acc = jnp.zeros((shots, 4 * k), jnp.float32)
+        for zz in range(zs):
+            acc = acc + dot_rows(buf[passing(x, zz)], rg[zz, : 4 * k])
+        zpart[i - 1, :shots] = half(acc)
+        partial_copy(i, x_at, projections, 1).start()
+
+    z = jnp.zeros((shots, 4 * k), jnp.float32)
+    for zz in range(zs):
+        z = z + dot_rows(col[zz], rg[zz, : 4 * k])
+    zacc[...] = z
     left, right = s_part[:, : 4 * k], s_part[:, 4 * k : 8 * k]
     for i in range(1, xs):
         x = (x_at + i) % xs
-        partial_copy(i, x).wait_recv()
-        z = z + zbuf[x, :shots].astype(jnp.float32)
+        partial_copy(i, x, grams, 0).wait_recv()
         left = left + zbuf[x, shots : shots + k].astype(jnp.float32)
         right = right + zbuf[x, shots + k :].astype(jnp.float32)
-
     s3t = half(left[:, :k])
     ss = half(right)
     f = left + dot(s3t, ss)
+    fb = f[:, 2 * k : 3 * k]
+    lift_map = f[:, 3 * k :] + dot_rows(half(fb), s3t)
+    lg[leaf, shots:] = half(-jnp.concatenate([f[:, k : 2 * k], lift_map], axis=1))
+
+    z = zacc[...]
+    for i in range(1, xs):
+        x = (x_at + i) % xs
+        partial_copy(i, x, projections, 1).wait_recv()
+        z = z + zbuf[x, :shots].astype(jnp.float32)
     proj = half(z[:, :k])
     zf = z + dot(proj, ss)
     carry, z2, z3 = zf[:, k : 2 * k], zf[:, 2 * k : 3 * k], zf[:, 3 * k :]
-    fb = f[:, 2 * k : 3 * k]
     lift = z3 + dot_rows(half(z2), s3t)
-    lift_map = f[:, 3 * k :] + dot_rows(half(fb), s3t)
     lg[leaf, :shots] = half(jnp.concatenate([carry, lift], axis=1))
-    lg[leaf, shots:] = half(-jnp.concatenate([f[:, k : 2 * k], lift_map], axis=1))
 
     def leaf_copy(i, frm):
         return pltpu.make_async_remote_copy(
@@ -317,7 +322,6 @@
     back_low[...] = jnp.concatenate([bl_ref[...], bc], axis=0)
 
     one_hot(steps // 2, steps)
-    bt[...] = b_ref[...].T
 
     for i in range(1, leaves):
         leaf_copy(i, (leaf + i) % leaves).wait_recv()
@@ -448,7 +452,8 @@
         leaf_copy(i, leaf).wait_send()
         grad_copy(i, leaf).wait_send()
     for i in range(1, xs):
-        partial_copy(i, x_at).wait_send()
+        partial_copy(i, x_at, grams, 0).wait_send()
+        partial_copy(i, x_at, projections, 1).wait_send()
 
         @pl.loop(0, zs)
         def _(d):
@@ -476,6 +481,7 @@
     anywhere = pl.BlockSpec(memory_space=pl.ANY)
     vmem = pl.BlockSpec(memory_space=pltpu.VMEM)
     vectors = max(zs * (xs - 1), 1)
+    parts = 4 if shots % 64 == 0 else 1
     small = pltpu.VMEM((k, block), bf16)
     solution_out, grad = pl.pallas_call(
         functools.partial(kernel, n, leaves, xs),
@@ -507,11 +513,11 @@
             pltpu.VMEM((n, slab, LANES), f32),
             pltpu.VMEM((leaves, slab, LANES), f32),
             dma((5,)), dma((zs,)),
-            dma((2, zs + 1)), dma((2, zs)),
+            dma((parts, zs + 1)), dma((parts, zs)),
             dma((vectors,)), dma((zs,)), dma((vectors,)), dma((2 * n,)),
-            dma((xs,)), dma((xs,)),
+            dma((2, xs)), dma((2, xs)),
             dma((leaves,)), dma((leaves,)),
-            dma((2, zs + 1)), dma((2, vectors)), dma((2, n)),
+            dma((parts, zs + 1)), dma((parts, vectors)), dma((parts, n)),
             dma((n,)), dma((n,)),
             dma((leaves,)), dma((leaves,)),
         ],

time: 99.6 us -> 98.5 us (0.989)
  Pallas kernels: 95.1 us -> 94 us
    pallas_call x1, Pallas kernels: 95.1 us -> 94 us  [per_device(): pl.pallas_call(functools.partial(kernel, n, leaves, xs), out_shape=(jax.S...]
where the time goes in v7:
time: 98.5 us; the launch traced here: 98.3 us
  Pallas kernels  94 us (95%)
  local copies, waits for them, and re-layouts  3.65 us (4%)
    pallas_call x1, Pallas kernels, per_device(): pl.pallas_call(functools.partial(kernel, n, leaves, xs), out_shape=(jax.S...  94 us
    unnamed x4, local copies, waits for them, and re-layouts  3.65 us

profile of v7, /device:TPU:0, one launch (start us, length us, event | category | flops | bytes accessed | tf_op | source)
XLA Modules:
  0.0 98.3 jit_solution(13348181351796067765)
XLA Ops:
  0.6 94.0 %shard_map.95 = (bf16[2048,512]{1,0:T(8,128)(2,1)}, f32[16,128]{1,0:T(8,128)}) custom-call(bf16[256,4096]{1,0:T(8,128)(2,1)} %src.1, bf16[512,512]{1,0:T(8,128)(2,1)} %b_hbm.1, bf16[64,512]{1,0:T(8,128)(2,1)} %bl_hbm.1, bf16[64,512]{1,0:T(8,128)(2,1)} %br_hbm.1, bf16[64,512]{1,0:T(8,128)(2,1)} %ci_hbm.1, bf16[64,512]{1,0:T(8,128)(2,1)} %co_hbm.1, ...), custom_call_target="tpu_custom_call" | custom-call | tf_op jit(solution)/shard_map/pallas_call | solution.py:486
  94.6 0.0 copy-start
  94.6 3.0 %copy.12 = bf16[2048,512]{1,0:T(8,128)(2,1)} copy(bf16[2048,512]{1,0:T(8,128)(2,1)} %get-tuple-element.8) | data formatting | bytes 4194304
  97.7 0.0 copy-done
  97.7 0.6 copy.13
Async XLA Ops:
  94.6 3.1 %copy-start = (f32[16,128]{1,0:T(8,128)S(1)}, f32[16,128]{1,0:T(8,128)}, u32[]{:S(2)}) copy-start(f32[16,128]{1,0:T(8,128)} %get-tuple-element.5) | copy-start | bytes 24580

commit v8 on v7

--- a/solution.py
+++ b/solution.py
@@ -186,6 +186,18 @@
         slot = passing(x, zz)
         return send(buf.at[slot], z_at * xs + x, f_send.at[(i - 1) * zs + d], zz * xs + x_at)
 
+    pl.semaphore_wait(barrier, n - 1 + leaves - 1)
+
+    for i in range(1, xs):
+        @pl.loop(1, zs + 1)
+        def _(d):
+            over_x(i, d % zs).start()
+
+    for zz in range(zs):
+        column_copy(zz).wait()
+    if zs > 1:
+        own_over_z(1).start()
+
     for c in loads:
         c.wait()
     b = b_ref[...]
@@ -200,22 +212,10 @@
     rg[z_at, 4 * k :, 4 * k : 8 * k] = half(
         dot_rows(br_ref[...], jnp.concatenate([bl_ref[...], stacked], axis=0))
     )
-    pl.semaphore_wait(barrier, n - 1 + leaves - 1)
-
     parts = rz.shape[0]
     basis = [Tree(rg, p, parts, rz, None, rr, leaf, node, zs, xs) for p in range(parts)]
     for part in basis:
         part.start()
-
-    for i in range(1, xs):
-        @pl.loop(1, zs + 1)
-        def _(d):
-            over_x(i, d % zs).start()
-
-    for zz in range(zs):
-        column_copy(zz).wait()
-    if zs > 1:
-        own_over_z(1).start()
 
     rows_at = min(256, total)
     steps = total // rows_at
@@ -233,10 +233,8 @@
     for hop in range(1, zs):
         for part in basis:
             part.relay(hop)
-        if hop == max(zs - 2, 1):
-            @pl.loop(2, zs)
-            def _(d):
-                own_over_z(d).start()
+        if hop + 1 < zs:
+            own_over_z(hop + 1).start()
 
     early, late = 1 + (zs - 1) // 3, 1 + 2 * (zs - 1) // 3
     for i in range(1, xs):

time: 98.5 us -> 99.2 us (level)
  no operation moved by 1% of the time
where the time goes in v8:
time: 99.2 us; the launch traced here: 99 us
  Pallas kernels  94.7 us (95%)
  local copies, waits for them, and re-layouts  3.65 us (4%)
    pallas_call x1, Pallas kernels, per_device(): pl.pallas_call(functools.partial(kernel, n, leaves, xs), out_shape=(jax.S...  94.7 us
    unnamed x4, local copies, waits for them, and re-layouts  3.65 us

profile of v8, /device:TPU:0, one launch (start us, length us, event | category | flops | bytes accessed | tf_op | source)
XLA Modules:
  0.0 99.0 jit_solution(6087594383998094800)
XLA Ops:
  0.6 94.7 %shard_map.95 = (bf16[2048,512]{1,0:T(8,128)(2,1)}, f32[16,128]{1,0:T(8,128)}) custom-call(bf16[256,4096]{1,0:T(8,128)(2,1)} %src.1, bf16[512,512]{1,0:T(8,128)(2,1)} %b_hbm.1, bf16[64,512]{1,0:T(8,128)(2,1)} %bl_hbm.1, bf16[64,512]{1,0:T(8,128)(2,1)} %br_hbm.1, bf16[64,512]{1,0:T(8,128)(2,1)} %ci_hbm.1, bf16[64,512]{1,0:T(8,128)(2,1)} %co_hbm.1, ...), custom_call_target="tpu_custom_call" | custom-call | tf_op jit(solution)/shard_map/pallas_call | solution.py:484
  95.3 0.0 copy-start
  95.4 3.0 %copy.12 = bf16[2048,512]{1,0:T(8,128)(2,1)} copy(bf16[2048,512]{1,0:T(8,128)(2,1)} %get-tuple-element.8) | data formatting | bytes 4194304
  98.4 0.0 copy-done
  98.4 0.6 copy.13
Async XLA Ops:
  95.3 3.1 %copy-start = (f32[16,128]{1,0:T(8,128)S(1)}, f32[16,128]{1,0:T(8,128)}, u32[]{:S(2)}) copy-start(f32[16,128]{1,0:T(8,128)} %get-tuple-element.5) | copy-start | bytes 24580

commit v9 on v8

--- a/solution.py
+++ b/solution.py
@@ -114,10 +114,10 @@
     n, leaves, xs,
     src, b_hbm, bl_hbm, br_hbm, ci_hbm, co_hbm, shot_ref, cell_ref,
     sol_ref, grad_ref,
-    b_ref, bl_ref, br_ref, ci_ref, co_ref, bt, col, buf, rg, zpart, zbuf, lg, cg,
+    b_ref, bl_ref, br_ref, ci_ref, co_ref, bt, col, buf, rg, zpart, zbuf, lg, early_c, late_c,
     fwd_low, back_low, onehot, sols, zacc, u_ref, t_ref, sums, gpart, gbuf, lbuf,
     in_sem, col_sem, rz, rr, x_send, o_send, f_send, a_recv, z_send, z_recv,
-    l_send, l_recv, cz, cx, cr, g_send, g_recv, h_send, h_recv,
+    l_send, l_recv, cz, cx, cr, dz, dx, dr, g_send, g_recv, h_send, h_recv,
 ):
     leaf, node = lax.axis_index("leaf"), lax.axis_index("node")
     zs = n // xs
@@ -233,8 +233,10 @@
     for hop in range(1, zs):
         for part in basis:
             part.relay(hop)
-        if hop + 1 < zs:
-            own_over_z(hop + 1).start()
+        if hop == max(zs - 2, 1):
+            @pl.loop(2, zs)
+            def _(d):
+                own_over_z(d).start()
 
     early, late = 1 + (zs - 1) // 3, 1 + 2 * (zs - 1) // 3
     for i in range(1, xs):
@@ -293,6 +295,7 @@
     proj = half(z[:, :k])
     zf = z + dot(proj, ss)
     carry, z2, z3 = zf[:, k : 2 * k], zf[:, 2 * k : 3 * k], zf[:, 3 * k :]
+    early_c[node] = half(jnp.concatenate([z[:, :k], z2], axis=1))
     lift = z3 + dot_rows(half(z2), s3t)
     lg[leaf, :shots] = half(jnp.concatenate([carry, lift], axis=1))
 
@@ -305,6 +308,10 @@
 
     for i in range(1, leaves):
         leaf_copy(i, leaf).start()
+    halves = cz.shape[0]
+    first = [Tree(early_c, p, halves, cz, cx, cr, leaf, node, zs, xs) for p in range(halves)]
+    for part in first:
+        part.start()
     for i in range(1, xs):
         @pl.loop(early, late)
         def _(d):
@@ -316,10 +323,16 @@
         t_ref[...]
         + lax.dot_general(s1, bl_ref[...], (((0,), (0,)), ((), ())), preferred_element_type=jnp.float32)
     )
-    fwd_low[...] = jnp.concatenate([br_ref[...], fc], axis=0)
-    back_low[...] = jnp.concatenate([bl_ref[...], bc], axis=0)
+    none = jnp.zeros_like(fc)
+    fb_low = half(dot(half(fb), bl_ref[...]))
+    fwd_low[...] = jnp.concatenate([br_ref[...], none, fc, none], axis=0)
+    back_low[...] = jnp.concatenate([none, bl_ref[...], fb_low, bc], axis=0)
 
     one_hot(steps // 2, steps)
+
+    for hop in range(1, min(zs, 2)):
+        for part in first:
+            part.relay(hop)
 
     for i in range(1, leaves):
         leaf_copy(i, (leaf + i) % leaves).wait_recv()
@@ -342,14 +355,14 @@
             returning = lifts[g] + dot_rows(half(returning), lg[g, shots:, :k])
         else:
             returning = lifts[g]
-    proj_fwd = z2 - dot(half(own_in), half(fb))
-    cg[node] = half(
-        jnp.concatenate([z[:, :k], -own_in, proj_fwd, -own_ret], axis=1)
-    )
-
-    coefs = [Tree(cg, p, parts, cz, cx, cr, leaf, node, zs, xs) for p in range(parts)]
+    late_c[node] = half(jnp.concatenate([-own_in, -own_ret], axis=1))
+
+    coefs = [Tree(late_c, p, halves, dz, dx, dr, leaf, node, zs, xs) for p in range(halves)]
     for part in coefs:
         part.start()
+    for hop in range(2, zs):
+        for part in first:
+            part.relay(hop)
     for hop in range(1, zs):
         for part in coefs:
             part.relay(hop)
@@ -358,15 +371,15 @@
                 @pl.loop(late, zs)
                 def _(d):
                     onward(i, d).start()
-    for part in coefs:
+    for part in first + coefs:
         part.partners()
 
     sums[...] = jnp.zeros_like(sums)
 
     def shot_block(j, rhs):
-        low = cg[j]
-        fwd = half(dot(rhs, b_ref[...]) + dot(low[:, : 2 * k], fwd_low[...]))
-        sol = half(dot(fwd, bt[...]) + dot(low[:, 2 * k :], back_low[...]))
+        low = jnp.concatenate([early_c[j], late_c[j]], axis=1)
+        fwd = half(dot(rhs, b_ref[...]) + dot(low, fwd_low[...]))
+        sol = half(dot(fwd, bt[...]) + dot(low, back_low[...]))
         sols[pl.ds(pl.multiple_of(j * shots, shots), shots), :] = sol
         sums[...] += jnp.sum(
             sol.astype(jnp.float32) * fwd.astype(jnp.float32), axis=0, keepdims=True
@@ -444,7 +457,7 @@
     grad_ref[...] = acc
 
 
-    for part in basis + coefs:
+    for part in basis + first + coefs:
         part.finish()
     for i in range(1, leaves):
         leaf_copy(i, leaf).wait_send()
@@ -479,6 +492,7 @@
     anywhere = pl.BlockSpec(memory_space=pl.ANY)
     vmem = pl.BlockSpec(memory_space=pltpu.VMEM)
     vectors = max(zs * (xs - 1), 1)
+    halves = 2 if shots % 32 == 0 else 1
     parts = 4 if shots % 64 == 0 else 1
     small = pltpu.VMEM((k, block), bf16)
     solution_out, grad = pl.pallas_call(
@@ -498,9 +512,10 @@
             pltpu.VMEM((max(xs - 1, 1), shots + 2 * k, 4 * k), bf16),
             pltpu.VMEM((xs, shots + 2 * k, 4 * k), bf16),
             pltpu.VMEM((leaves, shots + k, 2 * k), bf16),
-            pltpu.VMEM((n, shots, 4 * k), bf16),
-            pltpu.VMEM((2 * k, block), bf16),
-            pltpu.VMEM((2 * k, block), bf16),
+            pltpu.VMEM((n, shots, 2 * k), bf16),
+            pltpu.VMEM((n, shots, 2 * k), bf16),
+            pltpu.VMEM((4 * k, block), bf16),
+            pltpu.VMEM((4 * k, block), bf16),
             pltpu.VMEM((total, total), bf16),
             pltpu.VMEM((total, block), bf16),
             pltpu.VMEM((shots, 4 * k), f32),
@@ -515,7 +530,8 @@
             dma((vectors,)), dma((zs,)), dma((vectors,)), dma((2 * n,)),
             dma((2, xs)), dma((2, xs)),
             dma((leaves,)), dma((leaves,)),
-            dma((parts, zs + 1)), dma((parts, vectors)), dma((parts, n)),
+            dma((halves, zs + 1)), dma((halves, vectors)), dma((halves, n)),
+            dma((halves, zs + 1)), dma((halves, vectors)), dma((halves, n)),
             dma((n,)), dma((n,)),
             dma((leaves,)), dma((leaves,)),
         ],

time: 99.2 us -> 99.6 us (level)
  no operation moved by 1% of the time
where the time goes in v9:
time: 99.6 us; the launch traced here: 99.4 us
  Pallas kernels  95.1 us (95%)
  local copies, waits for them, and re-layouts  3.65 us (4%)
    pallas_call x1, Pallas kernels, per_device(): pl.pallas_call(functools.partial(kernel, n, leaves, xs), out_shape=(jax.S...  95.1 us
    unnamed x4, local copies, waits for them, and re-layouts  3.65 us

profile of v9, /device:TPU:0, one launch (start us, length us, event | category | flops | bytes accessed | tf_op | source)
XLA Modules:
  0.0 99.4 jit_solution(16096402185733498188)
XLA Ops:
  0.6 95.1 %shard_map.95 = (bf16[2048,512]{1,0:T(8,128)(2,1)}, f32[16,128]{1,0:T(8,128)}) custom-call(bf16[256,4096]{1,0:T(8,128)(2,1)} %src.1, bf16[512,512]{1,0:T(8,128)(2,1)} %b_hbm.1, bf16[64,512]{1,0:T(8,128)(2,1)} %bl_hbm.1, bf16[64,512]{1,0:T(8,128)(2,1)} %br_hbm.1, bf16[64,512]{1,0:T(8,128)(2,1)} %ci_hbm.1, bf16[64,512]{1,0:T(8,128)(2,1)} %co_hbm.1, ...), custom_call_target="tpu_custom_call" | custom-call | tf_op jit(solution)/shard_map/pallas_call | solution.py:498
  95.7 0.0 copy-start
  95.7 3.0 %copy.12 = bf16[2048,512]{1,0:T(8,128)(2,1)} copy(bf16[2048,512]{1,0:T(8,128)(2,1)} %get-tuple-element.8) | data formatting | bytes 4194304
  98.8 0.0 copy-done
  98.8 0.6 copy.13
Async XLA Ops:
  95.7 3.1 %copy-start = (f32[16,128]{1,0:T(8,128)S(1)}, f32[16,128]{1,0:T(8,128)}, u32[]{:S(2)}) copy-start(f32[16,128]{1,0:T(8,128)} %get-tuple-element.5) | copy-start | bytes 24580

commit v10 on v9

--- a/solution.py
+++ b/solution.py
@@ -186,18 +186,6 @@
         slot = passing(x, zz)
         return send(buf.at[slot], z_at * xs + x, f_send.at[(i - 1) * zs + d], zz * xs + x_at)
 
-    pl.semaphore_wait(barrier, n - 1 + leaves - 1)
-
-    for i in range(1, xs):
-        @pl.loop(1, zs + 1)
-        def _(d):
-            over_x(i, d % zs).start()
-
-    for zz in range(zs):
-        column_copy(zz).wait()
-    if zs > 1:
-        own_over_z(1).start()
-
     for c in loads:
         c.wait()
     b = b_ref[...]
@@ -212,10 +200,22 @@
     rg[z_at, 4 * k :, 4 * k : 8 * k] = half(
         dot_rows(br_ref[...], jnp.concatenate([bl_ref[...], stacked], axis=0))
     )
+    pl.semaphore_wait(barrier, n - 1 + leaves - 1)
+
     parts = rz.shape[0]
     basis = [Tree(rg, p, parts, rz, None, rr, leaf, node, zs, xs) for p in range(parts)]
     for part in basis:
         part.start()
+
+    for i in range(1, xs):
+        @pl.loop(1, zs + 1)
+        def _(d):
+            over_x(i, d % zs).start()
+
+    for zz in range(zs):
+        column_copy(zz).wait()
+    if zs > 1:
+        own_over_z(1).start()
 
     rows_at = min(256, total)
     steps = total // rows_at
@@ -366,7 +366,7 @@
     for hop in range(1, zs):
         for part in coefs:
             part.relay(hop)
-        if hop == max(zs - 2, 1):
+        if hop == 1:
             for i in range(1, xs):
                 @pl.loop(late, zs)
                 def _(d):

time: 99.6 us -> 100 us (level)
  no operation moved by 1% of the time
where the time goes in v10:
time: 100 us; the launch traced here: 99.8 us
  Pallas kernels  95.5 us (96%)
  local copies, waits for them, and re-layouts  3.65 us (4%)
    pallas_call x1, Pallas kernels, per_device(): pl.pallas_call(functools.partial(kernel, n, leaves, xs), out_shape=(jax.S...  95.5 us
    unnamed x4, local copies, waits for them, and re-layouts  3.65 us

profile of v10, /device:TPU:0, one launch (start us, length us, event | category | flops | bytes accessed | tf_op | source)
XLA Modules:
  0.0 99.8 jit_solution(4779837849393870877)
XLA Ops:
  0.6 95.5 %shard_map.95 = (bf16[2048,512]{1,0:T(8,128)(2,1)}, f32[16,128]{1,0:T(8,128)}) custom-call(bf16[256,4096]{1,0:T(8,128)(2,1)} %src.1, bf16[512,512]{1,0:T(8,128)(2,1)} %b_hbm.1, bf16[64,512]{1,0:T(8,128)(2,1)} %bl_hbm.1, bf16[64,512]{1,0:T(8,128)(2,1)} %br_hbm.1, bf16[64,512]{1,0:T(8,128)(2,1)} %ci_hbm.1, bf16[64,512]{1,0:T(8,128)(2,1)} %co_hbm.1, ...), custom_call_target="tpu_custom_call" | custom-call | tf_op jit(solution)/shard_map/pallas_call | solution.py:498
  96.1 0.0 copy-start
  96.1 3.0 %copy.12 = bf16[2048,512]{1,0:T(8,128)(2,1)} copy(bf16[2048,512]{1,0:T(8,128)(2,1)} %get-tuple-element.8) | data formatting | bytes 4194304
  99.2 0.0 copy-done
  99.2 0.6 copy.13
Async XLA Ops:
  96.1 3.1 %copy-start = (f32[16,128]{1,0:T(8,128)S(1)}, f32[16,128]{1,0:T(8,128)}, u32[]{:S(2)}) copy-start(f32[16,128]{1,0:T(8,128)} %get-tuple-element.5) | copy-start | bytes 24580
